TPU v7x, 256 devices: a whole 4x4x8 slice. The times are simulated.
256 devices in a mesh: tok: 8 (over y, core), lat: 32 (over z, x).
Axes of the slice: x: 4, y: 4, z: 8, core: 2. Of those that a mesh axis runs over, the one named last changes fastest.
Arguments:
- tokens: bfloat16 [32768, 8192], P(('tok', 'lat')), may hold values from -6 to 6
- dec_bias: float32 [8192], replicated, may hold values from -3 to 3
- enc_weight: bfloat16 [4096, 8192], P('lat'), may hold values from -0.0625 to 0.0625
- enc_bias: float32 [4096], P('lat'), may hold values from -3 to 3
- dec_weight: bfloat16 [4096, 8192], P('lat'), may hold values from -0.75 to 0.75
- block_ids: int32 [32768, 1], P(('tok', 'lat')), may hold values from 0 to 63, as said below
- block_home: int32 [64], replicated, may hold values from 0 to 63, as said below
Outputs:
- enc_grad: float32 [4096, 8192], P('lat', 'tok')
- dec_grad: float32 [4096, 8192], P('lat', 'tok')
Inputs may be any that keep to these rules, and one draw needn't show every extreme that they name: `block_ids`: each row names 1 different blocks. The 128 names in the rows of one device (aligned groups of 128 rows) name each block at most 6 times; in every token group the blocks of one lat device are each named exactly 6 times by the rows of every device of the group. A permutation: block b has place block_home[b], held by lat device block_home[b] // 2.
All inputs are finite; a program needn't handle non-finite values.
Results may differ from a plain program's by a relative error of at most 0.0024.
Values may be sent and summed in bfloat16 or wider, within the bound.
No kernel may reach another device: no remote copies, remote signals or barrier semaphores. Data moves between devices by JAX's collectives and lax.ppermute only.
A program may use at most 128 MiB of HBM per device.

v0:
```python
import jax
import jax.numpy as jnp
from jax import lax
from jax.sharding import PartitionSpec as P


def fill_slots(rows_in, filled, source_row):
    taken = jnp.take(rows_in, source_row, axis=0)
    return jnp.where(filled[:, None], taken, jnp.zeros_like(taken))


def on_device(tokens, dec_bias, enc_weight, enc_bias, dec_weight, block_ids, block_home):
    rows_here = tokens.shape[0]
    width = tokens.shape[1]
    lat_count = lax.axis_size("lat")
    block_total = block_home.shape[0]
    per_device = block_total // lat_count
    block_width = enc_weight.shape[0] // per_device
    picks = block_ids.shape[1]
    capacity = 3 * rows_here * picks // block_total
    slot_total = block_total * capacity
    pair_total = rows_here * picks
    flat_ids = block_ids.reshape(-1)
    matches = flat_ids[:, None] == jnp.arange(block_total, dtype=jnp.int32)[None, :]
    places = jnp.sum(jnp.where(matches, block_home[None, :], 0), axis=1)
    order = jnp.arange(pair_total, dtype=jnp.int32)
    earlier = order[None, :] < order[:, None]
    same = flat_ids[:, None] == flat_ids[None, :]
    ranks = jnp.sum(jnp.logical_and(same, earlier), axis=1)
    positions = places * capacity + ranks
    slot_hits = positions[None, :] == jnp.arange(slot_total, dtype=jnp.int32)[:, None]
    filled = jnp.any(slot_hits, axis=1)
    source_row = jnp.sum(jnp.where(slot_hits, (order // picks)[None, :], 0), axis=1)
    centered = (tokens.astype(jnp.float32) - dec_bias).astype(jnp.bfloat16)
    slot_shape = (lat_count, per_device * capacity, width)
    outgoing = fill_slots(centered, filled, source_row).reshape(slot_shape)
    received = lax.all_to_all(outgoing, "lat", split_axis=0, concat_axis=0, tiled=True)
    arrived = received.reshape(lat_count, per_device, capacity, width)
    enc_blocks = enc_weight.reshape(per_device, block_width, width)
    dec_blocks = dec_weight.reshape(per_device, block_width, width)
    bias_blocks = enc_bias.reshape(per_device, block_width)
    preact = (
        jnp.einsum("sbcd,bld->sbcl", arrived, enc_blocks, preferred_element_type=jnp.float32)
        + bias_blocks[None, :, None, :]
    )
    squash = jax.nn.sigmoid(preact)
    latent = (preact * squash).astype(jnp.bfloat16)
    decoded = jnp.einsum(
        "sbcl,bld->sbcd", latent, dec_blocks, preferred_element_type=jnp.float32
    ).astype(jnp.bfloat16)
    returned = lax.all_to_all(
        decoded.reshape(slot_shape), "lat", split_axis=0, concat_axis=0, tiled=True
    )
    pair_terms = jnp.take(returned.reshape(slot_total, width), positions, axis=0).reshape(
        rows_here, picks, width
    )
    recon = dec_bias + jnp.sum(pair_terms.astype(jnp.float32), axis=1)
    error = ((recon - tokens.astype(jnp.float32)) / 32.0).astype(jnp.bfloat16)
    error_out = fill_slots(error, filled, source_row).reshape(slot_shape)
    error_in = lax.all_to_all(error_out, "lat", split_axis=0, concat_axis=0, tiled=True).reshape(
        lat_count, per_device, capacity, width
    )
    dlatent = jnp.einsum("sbcd,bld->sbcl", error_in, dec_blocks, preferred_element_type=jnp.float32)
    dpreact = (dlatent * squash * (1.0 + preact * (1.0 - squash))).astype(jnp.bfloat16)
    half = per_device * block_width
    enc_part = jnp.einsum(
        "sbcl,sbcd->bld", dpreact, arrived, preferred_element_type=jnp.float32
    ).reshape(half, width)
    dec_part = jnp.einsum(
        "sbcl,sbcd->bld", latent, error_in, preferred_element_type=jnp.float32
    ).reshape(half, width)
    enc_grad, dec_grad = (
        lax.psum_scatter(enc_part, "tok", scatter_dimension=1, tiled=True),
        lax.psum_scatter(dec_part, "tok", scatter_dimension=1, tiled=True),
    )
    return (enc_grad, dec_grad)


def solution(mesh):
    in_specs = (
        P(("tok", "lat"), None),
        P(),
        P("lat", None),
        P("lat"),
        P("lat", None),
        P(("tok", "lat"), None),
        P(),
    )
    out_specs = (P("lat", "tok"), P("lat", "tok"))
    return jax.shard_map(
        on_device, mesh=mesh, in_specs=in_specs, out_specs=out_specs, check_vma=False
    )
```

profile of v0, /device:TPU:6, one launch (start us, length us, event | category | flops | bytes accessed | tf_op | source)
XLA Modules:
  0.0 818.3 jit_solution(308663675506274216)
XLA Ops:
  7.2 0.0 copy-start
  7.2 1.0 convert_reduce_fusion
  8.2 0.8 select_reduce_fusion.1
  9.0 0.1 select_reduce_fusion
  9.1 0.1 fusion.10
  9.3 3.4 fusion
  12.6 16.7 %gather_fusion.1 = bf16[384,8192]{1,0:T(8,128)(2,1)} fusion(bf16[128,8192]{1,0:T(8,128)(2,1)} %fusion, s32[1024]{0:T(1024)S(1)} %pad_clamp_fusion.1), kind=kCustom, calls=%fused_computation.clone | custom fusion | bytes 12584448 | tf_op jit(solution)/shard_map/jit(_take)/gather | solution.py:8
  29.4 6.3 select_select_fusion.1
  35.6 8.5 %reshape.92 = bf16[32,12,8192]{2,1,0:T(8,128)(2,1)} reshape(bf16[384,8192]{1,0:T(8,128)(2,1)} %select_select_fusion.1) | data formatting | bytes 12582912 | tf_op jit(solution)/shard_map/reshape | solution.py:36
  44.2 0.0 copy-start.5
  44.2 12.1 %all-to-all-start = ((bf16[32,12,8192]{2,1,0:T(8,128)(2,1)}), bf16[32,12,8192]{2,1,0:T(8,128)(2,1)}, u32[]{:S(2)}, u32[]{:S(2)}) async-start(bf16[32,12,8192]{2,1,0:T(8,128)(2,1)} %reshape.92), calls=%async_computation | async-start | bytes 16777216 | tf_op jit(solution)/shard_map/all_to_all | solution.py:37
  56.3 0.0 copy-done.5
  56.3 0.1 add.83
  56.4 187.3 %all-to-all-done = bf16[32,12,8192]{2,1,0:T(8,128)(2,1)} async-done(((bf16[32,12,8192]{2,1,0:T(8,128)(2,1)}), bf16[32,12,8192]{2,1,0:T(8,128)(2,1)}, u32[]{:S(2)}, u32[]{:S(2)}) %all-to-all-start) | async-done | bytes 6291488 | tf_op jit(solution)/shard_map/all_to_all | solution.py:37
  243.7 0.0 copy-start.3
  243.7 7.0 copy.15
  250.7 0.0 copy-start.2
  250.7 0.0 copy-done.3
  250.7 1.8 fusion.5
  252.5 0.0 copy-done
  252.5 4.5 convolution_convert_fusion
  257.0 0.0 copy-done.2
  257.0 9.6 %copy.16 = bf16[32,12,8192]{2,1,0:T(8,128)(2,1)} copy(bf16[32,12,8192]{2,0,1:T(8,128)(2,1)} %bitcast.54) | data formatting | bytes 12582912 | tf_op jit(solution)/shard_map/reshape | solution.py:52
  266.6 16.0 %all-to-all-start.1 = ((bf16[32,12,8192]{2,1,0:T(8,128)(2,1)}), bf16[32,12,8192]{2,1,0:T(8,128)(2,1)}, u32[]{:S(2)}, u32[]{:S(2)}) async-start(bf16[32,12,8192]{2,1,0:T(8,128)(2,1)} %copy.16), calls=%async_computation.1 | async-start | bytes 16777216 | tf_op jit(solution)/shard_map/all_to_all | solution.py:51
  282.6 0.3 reduce-scatter.5.cloned.1.call-start
  282.8 189.4 %all-to-all-done.1 = bf16[32,12,8192]{2,1,0:T(8,128)(2,1)} async-done(((bf16[32,12,8192]{2,1,0:T(8,128)(2,1)}), bf16[32,12,8192]{2,1,0:T(8,128)(2,1)}, u32[]{:S(2)}, u32[]{:S(2)}) %all-to-all-start.1) | async-done | bytes 6291488 | tf_op jit(solution)/shard_map/all_to_all | solution.py:51
  472.3 8.7 %reshape.97 = bf16[384,8192]{1,0:T(8,128)(2,1)} reshape(bf16[32,12,8192]{2,1,0:T(8,128)(2,1)} %all-to-all-done.1) | data formatting | bytes 12582912 | tf_op jit(solution)/shard_map/reshape | solution.py:54
  481.0 0.0 copy-start.4
  481.0 8.7 %gather_fusion = bf16[128,8192]{1,0:T(8,128)(2,1)} fusion(bf16[384,8192]{1,0:T(8,128)(2,1)} %reshape.97, s32[1024]{0:T(1024)S(1)} %pad_clamp_fusion), kind=kCustom, calls=%fused_computation.2 | custom fusion | bytes 4194816 | tf_op jit(solution)/shard_map/jit(_take)/gather | solution.py:54
  489.7 0.0 copy-done.4
  489.7 4.5 fusion.2
  494.2 16.7 %gather_fusion.2 = bf16[384,8192]{1,0:T(8,128)(2,1)} fusion(bf16[128,8192]{1,0:T(8,128)(2,1)} %fusion.2, s32[1024]{0:T(1024)S(1)} %pad_clamp_fusion.1), kind=kCustom, calls=%fused_computation.1.clone | custom fusion | bytes 12584448 | tf_op jit(solution)/shard_map/jit(_take)/gather | solution.py:8
  511.0 6.3 select_select_fusion
  517.2 8.5 %reshape.98 = bf16[32,12,8192]{2,1,0:T(8,128)(2,1)} reshape(bf16[384,8192]{1,0:T(8,128)(2,1)} %select_select_fusion) | data formatting | bytes 12582912 | tf_op jit(solution)/shard_map/reshape | solution.py:59
  525.7 194.3 %all_to_all.15 = bf16[32,12,8192]{2,1,0:T(8,128)(2,1)} all-to-all(bf16[32,12,8192]{2,1,0:T(8,128)(2,1)} %reshape.98), channel_id=1, replica_groups=mesh['tok'=8,'lat'=32] {'lat'}, dimensions={0} | all-to-all | bytes 12582912 | tf_op jit(solution)/shard_map/all_to_all | solution.py:60
  720.0 6.8 copy.17
  726.9 0.0 copy-start.1
  726.9 3.8 fusion.15
  730.7 0.1 copy-done.1
  730.8 0.0 reduce-scatter.5.cloned.1.call-update
  730.8 0.0 reduce-scatter.3.cloned.1.call-start
  730.9 9.7 %fusion.7 = f32[2,64,8192,1]{2,1,3,0:T(8,128)} fusion(bf16[32,2,6,8192]{3,0,2,1:T(8,128)(2,1)} %bitcast.52, bf16[32,2,6,8192]{3,0,2,1:T(8,128)(2,1)} %bitcast.50, bf16[2,64,8192,1]{2,1,3,0:T(8,128)(2,1)S(1)} %bitcast.48, f32[32,2,6,64]{3,0,2,1:T(8,128)S(1)} %fusion.5), kind=kOutput, calls=%fused_computation.17 | convolution fusion | flops 805527552 | bytes 18972672 | tf_op jit(solution)/shard_map/sbcl,sbcd->bld/dot_general | solution.py:66
  740.5 0.0 reduce-scatter.3.cloned.1.call-update
  740.6 28.0 %reduce-scatter.5.cloned.1.call-done = f32[128,1024]{1,0:T(8,128)} async-done(((f32[128,8192]{1,0:T(8,128)}), f32[128,1024]{1,0:T(8,128)}) %reduce-scatter.5.cloned.1.call-update) | async-done | bytes 524304 | tf_op jit(solution)/shard_map/reduce_scatter | solution.py:74
  768.5 42.5 %reduce-scatter.3.cloned.1.call-done = f32[128,1024]{1,0:T(8,128)} async-done(((f32[128,8192]{1,0:T(8,128)}), f32[128,1024]{1,0:T(8,128)}) %reduce-scatter.3.cloned.1.call-update) | async-done | bytes 524304 | tf_op jit(solution)/shard_map/reduce_scatter | solution.py:73
  (6 shorter events, 0.0 us)
Async XLA Ops:
  7.2 245.3 %copy-start = (bf16[128,8192]{1,0:T(8,128)(2,1)S(1)}, bf16[128,8192]{1,0:T(8,128)(2,1)}, u32[]{:S(2)}) copy-start(bf16[128,8192]{1,0:T(8,128)(2,1)} %param.13) | copy-start | bytes 6291460
  44.2 12.1 %copy-start.5 = (f32[128]{0:T(128)S(1)}, f32[128]{0:T(128)}, u32[]{:S(2)}) copy-start(f32[128]{0:T(128)} %param.12) | copy-start | bytes 1540
  44.2 199.5 %all-to-all-start = ((bf16[32,12,8192]{2,1,0:T(8,128)(2,1)}), bf16[32,12,8192]{2,1,0:T(8,128)(2,1)}, u32[]{:S(2)}, u32[]{:S(2)}) async-start(bf16[32,12,8192]{2,1,0:T(8,128)(2,1)} %reshape.92), calls=%async_computation | async-start | bytes 16777216 | tf_op jit(solution)/shard_map/all_to_all | solution.py:37
  243.7 7.0 copy-start.3
  250.7 6.3 copy-start.2
  266.6 205.7 %all-to-all-start.1 = ((bf16[32,12,8192]{2,1,0:T(8,128)(2,1)}), bf16[32,12,8192]{2,1,0:T(8,128)(2,1)}, u32[]{:S(2)}, u32[]{:S(2)}) async-start(bf16[32,12,8192]{2,1,0:T(8,128)(2,1)} %copy.16), calls=%async_computation.1 | async-start | bytes 16777216 | tf_op jit(solution)/shard_map/all_to_all | solution.py:51
  282.6 486.0 %reduce-scatter.5.cloned.1.call-start = ((), (), s32[]{:S(2)}) async-start(), calls=%async_computation.6 | async-start | bytes 4718592 | tf_op jit(solution)/shard_map/reduce_scatter | solution.py:74
  481.0 8.7 %copy-start.4 = (f32[8192]{0:T(1024)S(1)}, f32[8192]{0:T(1024)}, u32[]{:S(2)}) copy-start(f32[8192]{0:T(1024)} %param.10) | copy-start | bytes 98308
  726.9 3.9 copy-start.1
  730.8 80.2 %reduce-scatter.3.cloned.1.call-start = ((), (), s32[]{:S(2)}) async-start(), calls=%async_computation.5 | async-start | bytes 4718592 | tf_op jit(solution)/shard_map/reduce_scatter | solution.py:73
Sparse Core Ops, SparseCore 0:
  730.9 37.5 reduce-scatter.4
  771.7 39.3 reduce-scatter.2
where the time goes:
time: 826 us; the launch traced here: 818 us
  waiting for transfers between devices  447 us (54%)
  blocking collectives  194 us (23%)
  local copies, waits for them, and re-layouts  91.6 us (11%)
  starting transfers between devices  28.4 us (3%)
  other arithmetic  22.5 us (3%)
  matrix products  19.8 us (2%)
  between operations  14.6 us (2%)
    all_to_all x1, blocking collectives, on_device(): lax.all_to_all(error_out, 'lat', split_axis=0, concat_axis=0, tiled=True)  194 us
    all_to_all x1, waiting for transfers between devices, on_device(): lax.all_to_all(decoded.reshape(slot_shape), 'lat', split_axis=0, concat_a...  189 us
    all_to_all x1, waiting for transfers between devices, on_device(): lax.all_to_all(outgoing, 'lat', split_axis=0, concat_axis=0, tiled=True)  187 us
    reduce_scatter x1, waiting for transfers between devices, on_device(): lax.psum_scatter(enc_part, 'tok', scatter_dimension=1, tiled=True)  42.5 us
    gather x2, local copies, waits for them, and re-layouts, fill_slots(): taken = jnp.take(rows_in, source_row, axis=0)  33.5 us
    reduce_scatter x1, waiting for transfers between devices, on_device(): lax.psum_scatter(dec_part, 'tok', scatter_dimension=1, tiled=True)  28 us
  transfers between devices with their start and end apart: 4, of which 4 were waited for; matrix products, arithmetic and copies ran while one was open for 1% of the time, Pallas kernels for 0%

commit v1 on v0

--- a/solution.py
+++ b/solution.py
@@ -31,11 +31,21 @@
     slot_hits = positions[None, :] == jnp.arange(slot_total, dtype=jnp.int32)[:, None]
     filled = jnp.any(slot_hits, axis=1)
     source_row = jnp.sum(jnp.where(slot_hits, (order // picks)[None, :], 0), axis=1)
-    centered = (tokens.astype(jnp.float32) - dec_bias).astype(jnp.bfloat16)
     slot_shape = (lat_count, per_device * capacity, width)
-    outgoing = fill_slots(centered, filled, source_row).reshape(slot_shape)
+    outgoing = fill_slots(tokens, filled, source_row).reshape(slot_shape)
     received = lax.all_to_all(outgoing, "lat", split_axis=0, concat_axis=0, tiled=True)
-    arrived = received.reshape(lat_count, per_device, capacity, width)
+    named = lax.all_to_all(
+        filled.astype(jnp.float32).reshape(lat_count, per_device * capacity),
+        "lat",
+        split_axis=0,
+        concat_axis=0,
+        tiled=True,
+    )
+    used = named.reshape(lat_count, per_device, capacity, 1) > 0.5
+    rows_in = received.reshape(lat_count, per_device, capacity, width)
+    arrived = jnp.where(
+        used, (rows_in.astype(jnp.float32) - dec_bias).astype(jnp.bfloat16), jnp.bfloat16(0)
+    )
     enc_blocks = enc_weight.reshape(per_device, block_width, width)
     dec_blocks = dec_weight.reshape(per_device, block_width, width)
     bias_blocks = enc_bias.reshape(per_device, block_width)
@@ -48,17 +58,9 @@
     decoded = jnp.einsum(
         "sbcl,bld->sbcd", latent, dec_blocks, preferred_element_type=jnp.float32
     ).astype(jnp.bfloat16)
-    returned = lax.all_to_all(
-        decoded.reshape(slot_shape), "lat", split_axis=0, concat_axis=0, tiled=True
-    )
-    pair_terms = jnp.take(returned.reshape(slot_total, width), positions, axis=0).reshape(
-        rows_here, picks, width
-    )
-    recon = dec_bias + jnp.sum(pair_terms.astype(jnp.float32), axis=1)
-    error = ((recon - tokens.astype(jnp.float32)) / 32.0).astype(jnp.bfloat16)
-    error_out = fill_slots(error, filled, source_row).reshape(slot_shape)
-    error_in = lax.all_to_all(error_out, "lat", split_axis=0, concat_axis=0, tiled=True).reshape(
-        lat_count, per_device, capacity, width
+    recon = dec_bias + decoded.astype(jnp.float32)
+    error_in = jnp.where(
+        used, ((recon - rows_in.astype(jnp.float32)) / 32.0).astype(jnp.bfloat16), jnp.bfloat16(0)
     )
     dlatent = jnp.einsum("sbcd,bld->sbcl", error_in, dec_blocks, preferred_element_type=jnp.float32)
     dpreact = (dlatent * squash * (1.0 + preact * (1.0 - squash))).astype(jnp.bfloat16)

time: 826 us -> 369 us (0.45)
  blocking collectives: 194 us -> 0 us
  waiting for transfers between devices: 447 us -> 265 us
  local copies, waits for them, and re-layouts: 91.6 us -> 34.1 us
  other arithmetic: 22.5 us -> 9.76 us
    all_to_all x1 -> x0, blocking collectives: 194 us -> none  [on_device(): lax.all_to_all(error_out, 'lat', split_axis=0, concat_axis=0, tiled=True)]
    all_to_all x1, waiting for transfers between devices: 189 us -> 0.01 us  [on_device(): lax.all_to_all(filled.astype(jnp.float32).reshape(lat_count, per_device *...]
    reshape x4 -> x0, local copies, waits for them, and re-layouts: 35.4 us -> none  [the longest x1 9.6 us: on_device(): decoded.reshape(slot_shape)]
    reduce_scatter x1, waiting for transfers between devices: 28 us -> 42.4 us  [on_device(): lax.psum_scatter(dec_part, 'tok', scatter_dimension=1, tiled=True)]
    reduce_scatter x1, waiting for transfers between devices: 42.5 us -> 33.3 us  [on_device(): lax.psum_scatter(enc_part, 'tok', scatter_dimension=1, tiled=True)]
    gather x1 -> x0, local copies, waits for them, and re-layouts: 8.69 us -> none  [on_device(): jnp.take(returned.reshape(slot_total, width), positions, axis=0)]
  transfers between devices with their start and end apart: 4 -> 4, of which waited for: 4 -> 3; matrix products, arithmetic and copies ran while one was open for 1% -> 11% of each run, Pallas kernels for 0% -> 0%
where the time goes in v1:
time: 369 us; the launch traced here: 368 us
  waiting for transfers between devices  265 us (72%)
  local copies, waits for them, and re-layouts  34.1 us (9%)
  matrix products  22.7 us (6%)
  starting transfers between devices  21.8 us (6%)
  between operations  14.2 us (4%)
  other arithmetic  9.76 us (3%)
    all_to_all x1, waiting for transfers between devices, on_device(): lax.all_to_all(outgoing, 'lat', split_axis=0, concat_axis=0, tiled=True)  190 us
    reduce_scatter x1, waiting for transfers between devices, on_device(): lax.psum_scatter(dec_part, 'tok', scatter_dimension=1, tiled=True)  42.4 us
    reduce_scatter x1, waiting for transfers between devices, on_device(): lax.psum_scatter(enc_part, 'tok', scatter_dimension=1, tiled=True)  33.3 us
    gather x2, local copies, waits for them, and re-layouts, fill_slots(): taken = jnp.take(rows_in, source_row, axis=0)  25.3 us
    all_to_all x1, starting transfers between devices, on_device(): lax.all_to_all(filled.astype(jnp.float32).reshape(lat_count, per_device *...  11.6 us
    all_to_all x1, starting transfers between devices, on_device(): lax.all_to_all(outgoing, 'lat', split_axis=0, concat_axis=0, tiled=True)  9.96 us
    dot_general x1, matrix products, on_device(): jnp.einsum('sbcl,sbcd->bld', dpreact, arrived, preferred_element_type=jnp...  9.78 us
    select_n x1, other arithmetic, fill_slots(): return jnp.where(filled[:, None], taken, jnp.zeros_like(taken))  7.62 us
  transfers between devices with their start and end apart: 4, of which 3 were waited for; matrix products, arithmetic and copies ran while one was open for 11% of the time, Pallas kernels for 0%

profile of v1, /device:TPU:6, one launch (start us, length us, event | category | flops | bytes accessed | tf_op | source)
XLA Modules:
  0.0 367.9 jit_solution(7948690130835505713)
XLA Ops:
  7.2 0.0 copy-start
  7.2 1.0 convert_reduce_fusion
  8.2 0.8 select_reduce_fusion.1
  9.0 0.2 fusion.23
  9.1 0.7 reshape.92
  9.8 11.6 %all-to-all-start = ((f32[32,1,12]{2,1,0:T(1,128)}), f32[32,1,12]{2,1,0:T(1,128)S(1)}, u32[]{:S(2)}, u32[]{:S(2)}) async-start(f32[32,1,12]{2,1,0:T(1,128)} %bitcast.1), calls=%async_computation | async-start | bytes 32768 | tf_op jit(solution)/shard_map/all_to_all | solution.py:37
  21.4 0.1 select_reduce_fusion
  21.5 0.1 broadcast_in_dim.76
  21.7 0.1 reduce_sum.34
  21.8 16.7 %gather_fusion = bf16[384,8192]{1,0:T(8,128)(2,1)} fusion(bf16[128,8192]{1,0:T(8,128)(2,1)} %param.7, s32[1024]{0:T(1024)S(1)} %pad_clamp_fusion), kind=kCustom, calls=%fused_computation | custom fusion | bytes 12584448 | tf_op jit(solution)/shard_map/jit(_take)/gather | solution.py:8
  38.5 8.6 %gather.7 = bf16[32,12,8192]{2,1,0:T(8,128)(2,1)} reshape(bf16[384,8192]{1,0:T(8,128)(2,1)} %gather_fusion) | data formatting | bytes 12582912 | tf_op jit(solution)/shard_map/jit(_take)/gather | solution.py:8
  47.1 7.6 %select_select_fusion = bf16[32,12,8192]{2,1,0:T(8,128)(2,1)} fusion(bf16[32,12,8192]{2,1,0:T(8,128)(2,1)} %gather.7, pred[32,12]{1,0:T(8,128)(4,1)S(1)} %compare_and_fusion, pred[32,12]{1,0:T(8,128)(4,1)S(1)} %broadcast_in_dim.76), kind=kLoop, calls=%fused_computation.8 | loop fusion | flops 6291456 | bytes 12583680 | tf_op jit(solution)/shard_map/jit(_where)/select_n | solution.py:9
  54.7 0.0 copy-start.4
  54.7 0.0 all-to-all-done
  54.7 10.0 %all-to-all-start.1 = ((bf16[32,12,8192]{2,1,0:T(8,128)(2,1)}), bf16[32,12,8192]{2,1,0:T(8,128)(2,1)}, u32[]{:S(2)}, u32[]{:S(2)}) async-start(bf16[32,12,8192]{2,1,0:T(8,128)(2,1)} %select_select_fusion), calls=%async_computation.1 | async-start | bytes 16777216 | tf_op jit(solution)/shard_map/all_to_all | solution.py:36
  64.7 0.2 reduce-scatter.3.cloned.1.call-start
  64.9 0.0 copy-done.4
  64.9 0.1 add.74
  65.0 0.1 copy.26
  65.2 0.0 copy-start.3
  65.2 189.6 %all-to-all-done.1 = bf16[32,12,8192]{2,1,0:T(8,128)(2,1)} async-done(((bf16[32,12,8192]{2,1,0:T(8,128)(2,1)}), bf16[32,12,8192]{2,1,0:T(8,128)(2,1)}, u32[]{:S(2)}, u32[]{:S(2)}) %all-to-all-start.1) | async-done | bytes 6291488 | tf_op jit(solution)/shard_map/all_to_all | solution.py:36
  254.8 0.0 copy-start.2
  254.8 7.0 %copy.27 = bf16[32,12,8192]{2,0,1:T(8,128)(2,1)S(1)} copy(bf16[32,12,8192]{2,1,0:T(8,128)(2,1)} %all-to-all-done.1) | data formatting | bytes 12582912 | tf_op jit(solution)/shard_map/all_to_all | solution.py:36
  261.8 0.0 copy-start.1
  261.8 0.0 copy-done.3
  261.8 0.0 copy-done.2
  261.8 1.9 fusion.16
  263.7 0.0 copy-done
  263.7 0.7 copy-done.1
  264.4 4.9 %fusion.3 = bf16[32,2,6,8192]{3,0,2,1:T(8,128)(2,1)} fusion(bf16[32,2,6,8192]{3,0,2,1:T(8,128)(2,1)S(1)} %bitcast.49, bf16[2,64,8192,1]{2,1,3,0:T(8,128)(2,1)S(1)} %bitcast.45, f32[8192]{0:T(1024)S(1)} %copy-done.3, pred[32,2,6]{0,2,1:T(8,128)(4,1)S(1)} %gt.16, f32[32,2,6,64]{3,0,2,1:T(8,128)S(1)} %fusion.16), kind=kOutput, calls=%fused_computation.7 | convolution fusion | flops 427941888 | bytes 14811520 | tf_op jit(solution)/shard_map/sbcl,bld->sbcd/dot_general | solution.py:58
  269.3 9.8 %fusion.5 = f32[2,64,8192,1]{2,1,3,0:T(8,128)} fusion(bf16[32,2,6,8192]{3,0,2,1:T(8,128)(2,1)} %bitcast.50, f32[8192]{0:T(1024)S(1)} %copy-done.3, pred[32,2,6]{0,2,1:T(8,128)(4,1)S(1)} %gt.16, bf16[32,2,6,8192]{3,0,2,1:T(8,128)(2,1)} %fusion.3, bf16[2,64,8192,1]{2,1,3,0:T(8,128)(2,1)S(1)} %bitcast.46, f32[32,2,6,64]{3,0,2,1:T(8,128)S(1)} %fusion.16), kind=kOutput, calls=%fused_computation.10 | convolution fusion | flops 818110464 | bytes 19005824 | tf_op jit(solution)/shard_map/sbcl,sbcd->bld/dot_general | solution.py:68
  279.1 0.0 reduce-scatter.3.cloned.1.call-update
  279.1 0.0 reduce-scatter.5.cloned.1.call-start
  279.2 6.1 %fusion.30 = f32[2,64,8192,1]{2,1,3,0:T(8,128)} fusion(bf16[32,2,6,8192]{3,0,2,1:T(8,128)(2,1)} %fusion.3, f32[32,2,6,64]{3,0,2,1:T(8,128)S(1)} %fusion.16), kind=kOutput, calls=%fused_computation.44 | convolution fusion | flops 402776064 | bytes 10584064 | tf_op jit(solution)/shard_map/sbcl,sbcd->bld/dot_general | solution.py:71
  285.3 0.0 reduce-scatter.5.cloned.1.call-update
  285.4 33.3 %reduce-scatter.3.cloned.1.call-done = f32[128,1024]{1,0:T(8,128)} async-done(((f32[128,8192]{1,0:T(8,128)}), f32[128,1024]{1,0:T(8,128)}) %reduce-scatter.3.cloned.1.call-update) | async-done | bytes 524304 | tf_op jit(solution)/shard_map/reduce_scatter | solution.py:75
  318.6 42.4 %reduce-scatter.5.cloned.1.call-done = f32[128,1024]{1,0:T(8,128)} async-done(((f32[128,8192]{1,0:T(8,128)}), f32[128,1024]{1,0:T(8,128)}) %reduce-scatter.5.cloned.1.call-update) | async-done | bytes 524304 | tf_op jit(solution)/shard_map/reduce_scatter | solution.py:76
  (7 shorter events, 0.1 us)
Async XLA Ops:
  7.2 256.5 %copy-start = (bf16[128,8192]{1,0:T(8,128)(2,1)S(1)}, bf16[128,8192]{1,0:T(8,128)(2,1)}, u32[]{:S(2)}) copy-start(bf16[128,8192]{1,0:T(8,128)(2,1)} %param.11) | copy-start | bytes 6291460
  9.8 44.9 %all-to-all-start = ((f32[32,1,12]{2,1,0:T(1,128)}), f32[32,1,12]{2,1,0:T(1,128)S(1)}, u32[]{:S(2)}, u32[]{:S(2)}) async-start(f32[32,1,12]{2,1,0:T(1,128)} %bitcast.1), calls=%async_computation | async-start | bytes 32768 | tf_op jit(solution)/shard_map/all_to_all | solution.py:37
  54.7 10.2 %copy-start.4 = (f32[128]{0:T(128)S(1)}, f32[128]{0:T(128)}, u32[]{:S(2)}) copy-start(f32[128]{0:T(128)} %param.10) | copy-start | bytes 1540
  54.7 200.1 %all-to-all-start.1 = ((bf16[32,12,8192]{2,1,0:T(8,128)(2,1)}), bf16[32,12,8192]{2,1,0:T(8,128)(2,1)}, u32[]{:S(2)}, u32[]{:S(2)}) async-start(bf16[32,12,8192]{2,1,0:T(8,128)(2,1)} %select_select_fusion), calls=%async_computation.1 | async-start | bytes 16777216 | tf_op jit(solution)/shard_map/all_to_all | solution.py:36
  64.7 253.9 %reduce-scatter.3.cloned.1.call-start = ((), (), s32[]{:S(2)}) async-start(), calls=%async_computation.4 | async-start | bytes 4718592 | tf_op jit(solution)/shard_map/reduce_scatter | solution.py:75
  65.2 196.6 %copy-start.3 = (f32[8192]{0:T(1024)S(1)}, f32[8192]{0:T(1024)}, u32[]{:S(2)}) copy-start(f32[8192]{0:T(1024)} %param.8) | copy-start | bytes 98308
  254.8 7.0 %copy-start.2 = (bf16[128,8192]{1,0:T(8,128)(2,1)S(1)}, bf16[128,8192]{1,0:T(8,128)(2,1)}, u32[]{:S(2)}) copy-start(bf16[128,8192]{1,0:T(8,128)(2,1)} %param.9) | copy-start | bytes 6291460
  261.8 2.7 copy-start.1
  279.1 81.9 %reduce-scatter.5.cloned.1.call-start = ((), (), s32[]{:S(2)}) async-start(), calls=%async_computation.5 | async-start | bytes 4718592 | tf_op jit(solution)/shard_map/reduce_scatter | solution.py:76
Sparse Core Ops, SparseCore 0:
  279.3 39.3 reduce-scatter.2
  321.8 39.2 reduce-scatter.4

commit v2 on v0

v2 whole, which is shorter than its diff:
```python
import functools

import jax
import jax.numpy as jnp
from jax import lax
from jax.experimental import pallas as pl
from jax.experimental.pallas import tpu as pltpu
from jax.sharding import PartitionSpec as P

BF = jnp.bfloat16
F32 = jnp.float32
I32 = jnp.int32

HALVES = 2
SLOTS = 4
DIRECT = 2 * SLOTS
LENT = 7
EXTRA = 128
STRIDE = 16
BIG = pltpu.CompilerParams(vmem_limit_bytes=52 * 2**20)


def mm(a, b):
    return jnp.dot(a, b, preferred_element_type=F32)


def mm_t(a, b):
    return lax.dot_general(a, b, (((1,), (1,)), ((), ())), preferred_element_type=F32)


def iota(shape, axis):
    return lax.broadcasted_iota(I32, shape, axis)


def slot_codes(lat_count, first):
    row = iota((lat_count * HALVES * SLOTS, 1), 0)
    inner = row % (HALVES * SLOTS)
    return (row // (HALVES * SLOTS)) * STRIDE + first + inner % SLOTS, inner // SLOTS


def pick(codes, half, row_codes):
    hit = (row_codes >> 1) == codes
    block = jnp.sum(jnp.where(hit, 1 + (row_codes & 1), 0), axis=1, keepdims=True)
    low = jnp.where(jnp.logical_and(hit, half == 0), 1.0, 0.0).astype(BF)
    high = jnp.where(jnp.logical_and(hit, half == 1), 1.0, 0.0).astype(BF)
    return low, high, block


def before(n):
    return (iota((n, n), 0) < iota((n, n), 1)).astype(F32).astype(BF)


def ranks_of(dest, lat_count):
    g, n = dest.shape
    members = (dest[:, None, :] == iota((g, lat_count, n), 1)).astype(F32)
    counts = mm(members.reshape(g * lat_count, n).astype(BF), before(n)).reshape(g, lat_count, n)
    return members, jnp.sum(members * counts, axis=1)


def first_kernel(lat_count, ids, home, tokens, chunk, lent):
    rows, width = tokens.shape
    part = width // HALVES
    total = home.shape[0]
    hit = iota((total, rows), 0) == ids[...]
    places = jnp.sum(jnp.where(hit, home[...], 0), axis=0, keepdims=True)
    dest, block = places >> 1, places & 1
    unused, rank = ranks_of(dest, lat_count)
    rank = rank.astype(I32)
    codes, half = slot_codes(lat_count, 0)
    low, high, meta = pick(codes, half, (dest * STRIDE + rank) * 2 + block)
    both = jnp.concatenate([low, high], axis=1)
    step = 1024
    for i in range(part // step):
        a = tokens[:, i * step : (i + 1) * step]
        b = tokens[:, part + i * step : part + (i + 1) * step]
        chunk[:, i * step : (i + 1) * step] = mm(both, jnp.concatenate([a, b], axis=0)).astype(BF)
    chunk[:, part:] = jnp.broadcast_to(meta.astype(F32), (meta.shape[0], EXTRA)).astype(BF)
    over = (rank >= DIRECT).astype(F32)
    order = mm(jnp.broadcast_to(over, (8, rows)).astype(BF), before(rows))[:1]
    list_row = iota((LENT + 1, rows), 0)
    take = jnp.logical_and(order.astype(I32) == list_row, over > 0.5)
    take = jnp.logical_and(take, list_row < LENT)
    take = jnp.where(take, 1.0, 0.0).astype(BF)
    for i in range(width // step):
        got = mm(take, tokens[:, i * step : (i + 1) * step])
        if i == 0:
            head = jnp.where(list_row == LENT, places.astype(F32), got[:, :rows])
            got = jnp.concatenate([head, got[:, rows:]], axis=1)
        lent[:, i * step : (i + 1) * step] = got.astype(BF)


def second_kernel(lat_count, group, tokens, loans, chunk, left):
    rows, width = tokens.shape
    part = width // HALVES
    groups = loans.shape[0] // (LENT + 1)
    me = group[0]
    heads = loans[:, :rows].astype(F32).reshape(groups, LENT + 1, rows)
    places = heads[:, LENT, :].astype(I32)
    dest, block = places >> 1, places & 1
    members, rank_f = ranks_of(dest, lat_count)
    rank = rank_f.astype(I32)
    over = rank >= DIRECT
    order = mm(over.astype(F32).astype(BF), before(rows)).astype(I32)
    listed = jnp.logical_and(over, order < LENT)
    count = jnp.sum(members, axis=2, keepdims=True)
    asked = jnp.sum(members * listed.astype(F32)[:, None, :], axis=2, keepdims=True)
    used = jnp.maximum(count, float(SLOTS))
    free = jnp.maximum(DIRECT - used, 0.0)
    my_group = iota((groups, 1, 1), 0)
    asked_before = []
    running = jnp.zeros((1, lat_count, 1), F32)
    free_total = jnp.zeros((1, lat_count, 1), F32)
    free_before = jnp.zeros((1, lat_count, 1), F32)
    for t in range(groups):
        asked_before.append(running)
        running = running + asked[t : t + 1]
        free_before = free_before + jnp.where(me > t, free[t : t + 1], 0.0)
        free_total = free_total + free[t : t + 1]
    mine = (my_group == me).astype(F32)
    my_free = jnp.sum(free * mine, axis=0, keepdims=True)
    my_used = jnp.sum(used * mine, axis=0, keepdims=True)

    def look(values):
        return jnp.sum(members * values, axis=1).astype(I32)

    place_in_pool = look(jnp.concatenate(asked_before, axis=0)) + rank - DIRECT
    placed = jnp.logical_and(listed, place_in_pool < look(free_total))
    at = place_in_pool - look(free_before)
    here = jnp.logical_and(placed, jnp.logical_and(at >= 0, at < look(my_free)))
    slot = look(my_used) + at
    lent_code = jnp.where(here, (dest * STRIDE + slot) * 2 + block, -1)
    list_row = iota((LENT + 1, rows), 0)
    columns = []
    for t in range(groups):
        chosen = jnp.logical_and(order[t : t + 1] == list_row, listed[t : t + 1])
        value = jnp.sum(jnp.where(chosen, lent_code[t : t + 1] + 1, 0), axis=1, keepdims=True) - 1
        columns.append(value)
    column = jnp.concatenate(columns, axis=0)
    size = groups * (LENT + 1)
    lent_row = jnp.sum(
        jnp.where(iota((size, size), 0) == iota((size, size), 1), column, 0), axis=0, keepdims=True
    )
    mine2 = (iota((groups, 1), 0) == me).astype(I32)
    own_code = jnp.sum(((dest * STRIDE + rank) * 2 + block) * mine2, axis=0, keepdims=True)
    missing = jnp.logical_and(over, jnp.logical_not(placed)).astype(I32)
    own_missing = jnp.sum(missing * mine2, axis=0, keepdims=True)
    left[...] = jnp.broadcast_to(jnp.where(own_missing > 0, own_code, -1), left.shape)
    flag = jnp.max(jnp.max(missing.astype(F32), axis=1, keepdims=True), axis=0, keepdims=True)
    codes, half = slot_codes(lat_count, SLOTS)
    low, high, meta = pick(codes, half, own_code)
    low2, high2, meta2 = pick(codes, half, lent_row)
    both = jnp.concatenate([low, high], axis=1)
    both2 = jnp.concatenate([low2, high2], axis=1)
    step = 1024
    for i in range(part // step):
        lo, hi = slice(i * step, (i + 1) * step), slice(part + i * step, part + (i + 1) * step)
        own = jnp.concatenate([tokens[:, lo], tokens[:, hi]], axis=0)
        other = jnp.concatenate([loans[:, lo], loans[:, hi]], axis=0)
        chunk[:, lo] = (mm(both, own) + mm(both2, other)).astype(BF)
    code = (meta + meta2).astype(F32) + 4.0 * flag
    chunk[:, part:] = jnp.broadcast_to(code, (code.shape[0], EXTRA)).astype(BF)


def gradient_body(chunk, enc, dec, bias, dec_bias, cent, err, acc, store):
    rows, padded = chunk.shape
    part = padded - EXTRA
    latents = enc.shape[0]
    step = 1024
    steps = part // step
    group = HALVES * SLOTS
    half = iota((rows, 1), 0) % group // SLOTS
    high_row = iota((group, 1), 0) // SLOTS == 1

    def pair(i):
        lo, hi = slice(i * step, (i + 1) * step), slice(part + i * step, part + (i + 1) * step)
        return lo, hi

    def offset(i):
        lo, hi = pair(i)
        return jnp.where(high_row, dec_bias[:, hi], dec_bias[:, lo])[None]

    def joined(total):
        own = jnp.where(half == 0, total[:, :latents], total[:, latents:])
        down = pltpu.roll(own, SLOTS, 0)
        up = pltpu.roll(own, rows - SLOTS, 0)
        return own + jnp.where(half == 0, up, down)

    def spread(values):
        zero = jnp.zeros_like(values)
        return jnp.concatenate(
            [jnp.where(half == 0, values, zero), jnp.where(half == 1, values, zero)], axis=1
        )

    for i in range(steps):
        lo, hi = pair(i)
        x = chunk[:, lo].astype(F32).reshape(rows // group, group, step)
        c = (x - offset(i)).reshape(rows, step).astype(BF)
        cent[:, lo] = c
        w = jnp.concatenate([enc[:, lo], enc[:, hi]], axis=0)
        if i == 0:
            acc[...] = mm_t(c, w)
        else:
            acc[...] += mm_t(c, w)
    code = chunk[:, part:].astype(F32)
    code = jnp.where(code >= 4.0, code - 4.0, code)
    second = iota((1, latents), 1) >= latents // 2
    valid = code == jnp.where(second, 2.0, 1.0)
    pre = joined(acc[...]) + bias[...]
    gate = 1.0 / (1.0 + jnp.exp(-pre))
    latent = spread(jnp.where(valid, pre * gate, 0.0))
    latent_b = latent.astype(BF)
    for i in range(steps):
        lo, hi = pair(i)
        w = jnp.concatenate([dec[:, lo], dec[:, hi]], axis=0)
        d = mm(latent_b, w).astype(BF).astype(F32).reshape(rows // group, group, step)
        x = chunk[:, lo].astype(F32).reshape(rows // group, group, step)
        e = ((offset(i) + d - x) * (1.0 / 32.0)).reshape(rows, step).astype(BF)
        err[:, lo] = e
        if i == 0:
            acc[...] = mm_t(e, w)
        else:
            acc[...] += mm_t(e, w)
    dlatent = joined(acc[...])
    dpre = spread(jnp.where(valid, dlatent * gate * (1.0 + pre * (1.0 - gate)), 0.0))
    dpre_t = dpre.T.astype(BF)
    latent_t = latent.T.astype(BF)
    for i in range(steps):
        lo, hi = pair(i)
        store(i, 0, mm(dpre_t, cent[:, lo]))
        store(i, 1, mm(latent_t, err[:, lo]))


def part_kernel(chunk, enc, dec, bias, dec_bias, parts, cent, err, acc):
    latents = enc.shape[0]
    steps = parts.shape[0] // HALVES

    def store(i, grad, value):
        rows = slice(grad * latents, (grad + 1) * latents)
        parts[i, rows] = value[:latents]
        parts[steps + i, rows] = value[latents:]

    gradient_body(chunk, enc, dec, bias, dec_bias, cent, err, acc, store)


def last_kernel(
    core, chunk, enc, dec, bias, dec_bias, parts, mine, other, flags, cent, err, acc
):
    latents = enc.shape[0]
    steps = parts.shape[0] // HALVES

    def store(i, grad, value):
        rows = slice(grad * latents, (grad + 1) * latents)
        for h in range(HALVES):
            k = h * steps + i
            total = value[h * latents : (h + 1) * latents] + parts[k, rows]

            @pl.when(core[0] == k % 2)
            def _():
                mine[k // 2, rows] = total

            @pl.when(core[0] != k % 2)
            def _():
                other[k // 2, rows] = total.astype(BF)

    top = jnp.max(chunk[:, chunk.shape[1] - EXTRA :].astype(F32), axis=0, keepdims=True)
    flags[...] = jnp.broadcast_to(top, flags.shape)
    gradient_body(chunk, enc, dec, bias, dec_bias, cent, err, acc, store)


def vmem():
    return pl.BlockSpec(memory_space=pltpu.VMEM)


def smem():
    return pl.BlockSpec(memory_space=pltpu.SMEM)


def on_device(tokens, dec_bias, enc_weight, enc_bias, dec_weight, block_ids, block_home):
    rows, width = tokens.shape
    lat_count = lax.axis_size("lat")
    groups = lax.axis_size("tok")
    part = width // HALVES
    slot_rows = lat_count * HALVES * SLOTS
    latents = enc_weight.shape[0]
    out_width = width // groups
    me = lax.axis_index("tok").astype(I32)
    chunk_shape = jax.ShapeDtypeStruct((slot_rows, part + EXTRA), BF)
    matmul_cost = pl.CostEstimate(
        flops=5 * 2 * slot_rows * 2 * latents * part, bytes_accessed=16 * 2**20, transcendentals=0
    )
    move_cost = pl.CostEstimate(
        flops=2 * slot_rows * 2 * rows * part, bytes_accessed=5 * 2**20, transcendentals=0
    )

    chunk1, lent = pl.pallas_call(
        functools.partial(first_kernel, lat_count),
        out_shape=[chunk_shape, jax.ShapeDtypeStruct((LENT + 1, width), BF)],
        in_specs=[vmem()] * 3,
        out_specs=[vmem()] * 2,
        compiler_params=BIG,
        cost_estimate=move_cost,
        name="first_slots",
    )(block_ids.reshape(1, rows), block_home.reshape(-1, 1), tokens)

    def exchange(chunk):
        shaped = chunk.reshape(lat_count, HALVES * SLOTS, part + EXTRA)
        got = lax.all_to_all(shaped, "lat", split_axis=0, concat_axis=0, tiled=True)
        return got.reshape(slot_rows, part + EXTRA)

    loans = lax.all_gather(lent, "tok", tiled=True)
    got1 = exchange(chunk1)
    chunk2, left = pl.pallas_call(
        functools.partial(second_kernel, lat_count),
        out_shape=[chunk_shape, jax.ShapeDtypeStruct((8, rows), I32)],
        in_specs=[smem(), vmem(), vmem()],
        out_specs=[vmem()] * 2,
        compiler_params=BIG,
        cost_estimate=move_cost,
        name="second_slots",
    )(me.reshape(1), tokens, loans)
    got2 = exchange(chunk2)

    bias_row = enc_bias.reshape(1, latents)
    offset_row = dec_bias.reshape(1, width)
    work = [
        pltpu.VMEM((slot_rows, part), BF),
        pltpu.VMEM((slot_rows, part), BF),
        pltpu.VMEM((slot_rows, HALVES * latents), F32),
    ]
    part_call = pl.pallas_call(
        part_kernel,
        out_shape=jax.ShapeDtypeStruct((groups, 2 * latents, out_width), F32),
        in_specs=[vmem()] * 5,
        out_specs=vmem(),
        scratch_shapes=work,
        compiler_params=BIG,
        cost_estimate=matmul_cost,
        name="chunk_gradients",
    )
    parts = part_call(got1, enc_weight, dec_weight, bias_row, offset_row)
    core = me % 2
    half_groups = groups // 2
    mine, other, flags = pl.pallas_call(
        last_kernel,
        out_shape=[
            jax.ShapeDtypeStruct((half_groups, 2 * latents, out_width), F32),
            jax.ShapeDtypeStruct((half_groups, 2 * latents, out_width), BF),
            jax.ShapeDtypeStruct((8, EXTRA), F32),
        ],
        in_specs=[smem()] + [vmem()] * 6,
        out_specs=[vmem()] * 3,
        scratch_shapes=work,
        compiler_params=BIG,
        cost_estimate=matmul_cost,
        name="last_gradients",
    )(core.reshape(1), got2, enc_weight, dec_weight, bias_row, offset_row, parts)

    def finish(mine, other):
        swapped = lax.ppermute(other, "tok", [(i, i ^ 1) for i in range(groups)])
        summed = (mine + swapped.astype(F32)).astype(BF)
        same_core = [[2 * i + c for i in range(half_groups)] for c in range(2)]
        terms = lax.all_to_all(
            summed, "tok", split_axis=0, concat_axis=0, tiled=True, axis_index_groups=same_core
        )
        total = jnp.sum(terms.astype(F32), axis=0)
        return total[:latents], total[latents:]

    def with_rest(mine, other):
        codes, half = slot_codes(lat_count, DIRECT)
        low, high, meta = pick(codes, half, left[:1])
        data = mm(low, tokens[:, :part]) + mm(high, tokens[:, part:])
        extra = jnp.broadcast_to(meta.astype(F32), (slot_rows, EXTRA))
        chunk3 = jnp.concatenate([data, extra], axis=1).astype(BF)
        rest = part_call(exchange(chunk3), enc_weight, dec_weight, bias_row, offset_row)
        rest = rest.reshape(half_groups, 2, 2 * latents, out_width)
        mine = mine + lax.dynamic_index_in_dim(rest, core, 1, keepdims=False)
        more = lax.dynamic_index_in_dim(rest, 1 - core, 1, keepdims=False)
        return finish(mine, (other.astype(F32) + more).astype(BF))

    return lax.cond(flags[0, 0] >= 4.0, with_rest, finish, mine, other)


def solution(mesh):
    in_specs = (
        P(("tok", "lat"), None),
        P(),
        P("lat", None),
        P("lat"),
        P("lat", None),
        P(("tok", "lat"), None),
        P(),
    )
    out_specs = (P("lat", "tok"), P("lat", "tok"))
    return jax.shard_map(
        on_device, mesh=mesh, in_specs=in_specs, out_specs=out_specs, check_vma=False
    )
```

time: 826 us -> 198 us (0.24)
  waiting for transfers between devices: 447 us -> 91 us
  blocking collectives: 194 us -> 30.9 us
  local copies, waits for them, and re-layouts: 91.6 us -> 5.41 us
  Pallas kernels: 0 us -> 32.8 us
  matrix products: 19.8 us -> 0 us
  other arithmetic: 22.5 us -> 4.47 us
  starting transfers between devices: 28.4 us -> 18.4 us
    all_to_all x2, waiting for transfers between devices: 377 us -> 56.4 us  [exchange(): got = lax.all_to_all(shaped, 'lat', split_axis=0, concat_axis=0, tiled=True)]
    all_to_all x1, blocking collectives: 194 us -> 30.9 us  [finish(): lax.all_to_all(summed, 'tok', split_axis=0, concat_axis=0, tiled=True, ax...]
    reduce_scatter x2 -> x0, waiting for transfers between devices: 70.4 us -> none  [the longest x1 42.5 us: on_device(): lax.psum_scatter(enc_part, 'tok', scatter_dimension=1, tiled=True)]
    gather x3 -> x0, local copies, waits for them, and re-layouts: 42.2 us -> none  [the longest x2 33.5 us: fill_slots(): taken = jnp.take(rows_in, source_row, axis=0)]
    reshape x4 -> x1, local copies, waits for them, and re-layouts: 35.4 us -> 0.75 us  [on_device(): block_home.reshape(-1, 1)]
    pallas_call x0 -> x4, Pallas kernels: none -> 32.8 us  [the longest x1 14.7 us: on_device(): pl.pallas_call(last_kernel, out_shape=[jax.ShapeDtypeStruct((half_groups,...]
    all_gather x0 -> x1, waiting for transfers between devices: none -> 29.6 us  [on_device(): loans = lax.all_gather(lent, 'tok', tiled=True)]
    dot_general x4 -> x0, matrix products: 19.8 us -> none  [the longest x1 9.7 us: on_device(): jnp.einsum('sbcl,sbcd->bld', dpreact, arrived, preferred_element_type=jnp...]
  transfers between devices with their start and end apart: 4 -> 4, of which waited for: 4 -> 4; matrix products, arithmetic and copies ran while one was open for 1% -> 0% of each run, Pallas kernels for 0% -> 7%
where the time goes in v2:
time: 198 us
  waiting for transfers between devices  91 us (46%)
  Pallas kernels  32.8 us (17%)
  blocking collectives  30.9 us (16%)
  starting transfers between devices  18.4 us (9%)
  between operations  14.7 us (7%)
  local copies, waits for them, and re-layouts  5.41 us (3%)
  other arithmetic  4.47 us (2%)
    all_to_all x2, waiting for transfers between devices, exchange(): got = lax.all_to_all(shaped, 'lat', split_axis=0, concat_axis=0, tiled=True)  56.4 us
    all_to_all x1, blocking collectives, finish(): lax.all_to_all(summed, 'tok', split_axis=0, concat_axis=0, tiled=True, ax...  30.9 us
    all_gather x1, waiting for transfers between devices, on_device(): loans = lax.all_gather(lent, 'tok', tiled=True)  29.6 us
    all_to_all x2, starting transfers between devices, exchange(): got = lax.all_to_all(shaped, 'lat', split_axis=0, concat_axis=0, tiled=True)  18.3 us
    pallas_call x1, Pallas kernels, on_device(): pl.pallas_call(last_kernel, out_shape=[jax.ShapeDtypeStruct((half_groups,...  14.7 us
    pallas_call x1, Pallas kernels, on_device(): parts = part_call(got1, enc_weight, dec_weight, bias_row, offset_row)  10.8 us
    ppermute x1, waiting for transfers between devices, finish(): swapped = lax.ppermute(other, 'tok', [(i, i ^ 1) for i in range(groups)])  4.36 us
  transfers between devices with their start and end apart: 4, of which 4 were waited for; matrix products, arithmetic and copies ran while one was open for 0% of the time, Pallas kernels for 7%

profile of v2, /device:TPU:6, one launch (start us, length us, event | category | flops | bytes accessed | tf_op | source)
XLA Modules:
  0.0 197.8 jit_solution(12532515817593255181)
XLA Ops:
  7.2 0.7 copy.11.home
  7.9 0.0 copy-start.1
  7.9 0.7 copy-done.1
  8.6 3.9 %first_slots.1 = (bf16[256,4224]{1,0:T(8,128)(2,1)}, bf16[8,8192]{1,0:T(8,128)(2,1)}) custom-call(s32[1,128]{1,0:T(1,128)S(1)} %bitcast.29, s32[64,1]{1,0:T(8,128)S(1)} %copy.11.home, bf16[128,8192]{1,0:T(8,128)(2,1)} %tokens.3), custom_call_target="tpu_custom_call" | custom-call | flops 536870912 | bytes 5242880 | tf_op jit(solution)/shard_map/first_slots/pallas_call | solution.py:295
  12.4 0.0 copy-start.2
  12.4 11.7 %all-to-all-start.4 = ((bf16[32,8,4224]{2,1,0:T(8,128)(2,1)}), bf16[32,8,4224]{2,1,0:T(8,128)(2,1)}, u32[]{:S(2)}, u32[]{:S(2)}) async-start(bf16[32,8,4224]{2,1,0:T(8,128)(2,1)} %bitcast.33), calls=%async_computation.4 | async-start | bytes 4325376 | tf_op jit(solution)/shard_map/all_to_all | solution.py:307
  24.2 0.0 all-gather.2.cloned.1.call-start
  24.2 0.7 all-gather.2.cloned.1.call-update
  24.9 29.6 %all-gather.2.cloned.1.call-done.loans = bf16[64,8192]{1,0:T(8,128)(2,1)} async-done(((bf16[8,8192]{1,0:T(8,128)(2,1)}), bf16[64,8192]{1,0:T(8,128)(2,1)}) %all-gather.2.cloned.1.call-update) | async-done | bytes 1048592 | tf_op jit(solution)/shard_map/all_gather | solution.py:310
  54.5 0.0 copy-done.2
  54.5 0.0 copy-start
  54.6 1.2 copy-done
  55.8 3.4 %second_slots.1 = (bf16[256,4224]{1,0:T(8,128)(2,1)}, s32[8,128]{1,0:T(8,128)S(1)}) custom-call(s32[1]{0:T(128)} %bitcast.8.group, bf16[128,8192]{1,0:T(8,128)(2,1)S(1)} %copy-done.2, bf16[64,8192]{1,0:T(8,128)(2,1)S(1)} %copy-done), custom_call_target="tpu_custom_call" | custom-call | flops 536870912 | bytes 5242880 | tf_op jit(solution)/shard_map/second_slots/pallas_call | solution.py:312
  59.2 16.2 %all-to-all-done.4 = bf16[32,8,4224]{2,1,0:T(8,128)(2,1)} async-done(((bf16[32,8,4224]{2,1,0:T(8,128)(2,1)}), bf16[32,8,4224]{2,1,0:T(8,128)(2,1)}, u32[]{:S(2)}, u32[]{:S(2)}) %all-to-all-start.4) | async-done | bytes 2162720 | tf_op jit(solution)/shard_map/all_to_all | solution.py:307
  75.4 0.0 copy-start.4
  75.4 0.0 copy-start.5
  75.4 6.5 %all-to-all-start.3 = ((bf16[32,8,4224]{2,1,0:T(8,128)(2,1)}), bf16[32,8,4224]{2,1,0:T(8,128)(2,1)}, u32[]{:S(2)}, u32[]{:S(2)}) async-start(bf16[32,8,4224]{2,1,0:T(8,128)(2,1)} %bitcast.32), calls=%async_computation.3 | async-start | bytes 4325376 | tf_op jit(solution)/shard_map/all_to_all | solution.py:307
  82.0 0.0 copy-done.4
  82.0 0.0 copy-done.5
  82.0 10.8 %chunk_gradients.3.parts = f32[8,256,1024]{2,1,0:T(8,128)} custom-call(bf16[256,4224]{1,0:T(8,128)(2,1)} %bitcast.16.chunk, bf16[128,8192]{1,0:T(8,128)(2,1)} %enc.3, bf16[128,8192]{1,0:T(8,128)(2,1)} %dec.3, f32[1,128]{1,0:T(1,128)S(1)} %bitcast.37, f32[1,8192]{1,0:T(1,128)S(1)} %bitcast.34), custom_call_target="tpu_custom_call" | custom-call | flops 2684354560 | bytes 16777216 | tf_op jit(solution)/shard_map/chunk_gradients/pallas_call | solution.py:340
  92.8 40.2 %all-to-all-done.3 = bf16[32,8,4224]{2,1,0:T(8,128)(2,1)} async-done(((bf16[32,8,4224]{2,1,0:T(8,128)(2,1)}), bf16[32,8,4224]{2,1,0:T(8,128)(2,1)}, u32[]{:S(2)}, u32[]{:S(2)}) %all-to-all-start.3) | async-done | bytes 2162720 | tf_op jit(solution)/shard_map/all_to_all | solution.py:307
  133.0 14.7 %last_gradients.1 = (f32[4,256,1024]{2,1,0:T(8,128)}, bf16[4,256,1024]{2,1,0:T(8,128)(2,1)}, f32[8,128]{1,0:T(8,128)S(1)}) custom-call(s32[1]{0:T(128)} %bitcast.7.core, bf16[256,4224]{1,0:T(8,128)(2,1)} %bitcast.12.chunk, bf16[128,8192]{1,0:T(8,128)(2,1)} %enc.3, bf16[128,8192]{1,0:T(8,128)(2,1)} %dec.3, f32[1,128]{1,0:T(1,128)S(1)} %bitcast.38, ...), custom_call_target="tpu_custom_call" | custom-call | flops 2684354560 | bytes 16777216 | tf_op jit(solution)/shard_map/last_gradients/pallas_call | solution.py:343
  147.6 0.5 slice.24
  148.8 41.1 %conditional.1 = (f32[256,1024]{1,0:T(8,128)}, f32[256,1024]{1,0:T(8,128)S(1)}) conditional(s32[]{:T(128)} %bitcast.17, (bf16[4,256,1024]{2,1,0:T(8,128)(2,1)}, f32[4,256,1024]{2,1,0:T(8,128)}) %tuple.15, (s32[8,128]{1,0:T(8,128)S(1)}, bf16[128,8192]{1,0:T(8,128)(2,1)S(1)}, bf16[128,8192]{1,0:T(8,128)(2,1)}, bf16[128,8192]{1,0:T(8,128)(2,1)}, ...), branch_computations={%region_0.2_spmd, %region_2.5_spmd} | conditional | flops 3237201920 | bytes 87438536 | solution.py:380
  148.8 0.1 collective-permute-start
  148.9 4.4 %collective-permute-done = bf16[4,256,1024]{2,1,0:T(8,128)(2,1)S(1)} collective-permute-done((bf16[4,256,1024]{2,1,0:T(8,128)(2,1)}, bf16[4,256,1024]{2,1,0:T(8,128)(2,1)S(1)}, u32[]{:S(2)}, u32[]{:S(2)}) %collective-permute-start) | collective-permute-done | bytes 2097184 | tf_op jit(solution)/shard_map/cond/branch_0_fun/ppermute | solution.py:359
  153.3 3.0 %add_convert_fusion = bf16[4,256,1024]{2,1,0:T(8,128)(2,1)S(1)} fusion(f32[4,256,1024]{2,1,0:T(8,128)} %get-tuple-element.22, bf16[4,256,1024]{2,1,0:T(8,128)(2,1)S(1)} %collective-permute-done), kind=kLoop, calls=%fused_computation.1 | loop fusion | flops 3145728 | bytes 8388608 | tf_op jit(solution)/shard_map/cond/branch_0_fun/convert_element_type | solution.py:360
  156.3 30.9 %all_to_all.22 = bf16[4,256,1024]{2,1,0:T(8,128)(2,1)S(1)} all-to-all(bf16[4,256,1024]{2,1,0:T(8,128)(2,1)S(1)} %add_convert_fusion), channel_id=1, replica_groups={{0,64,128,192},{32,96,160,224},{1,65,129,193},{33,97,161,225},{2,66,130..., dimensions={0} | all-to-all | bytes 4194304 | tf_op jit(solution)/shard_map/cond/branch_0_fun/all_to_all | solution.py:362
  187.2 1.4 convert_reduce_fusion
  188.7 1.2 copy.18
  189.9 1.0 fusion.28
Async XLA Ops:
  7.9 0.7 copy-start.1
  12.4 42.1 %copy-start.2 = (bf16[128,8192]{1,0:T(8,128)(2,1)S(1)}, bf16[128,8192]{1,0:T(8,128)(2,1)}, u32[]{:S(2)}) copy-start(bf16[128,8192]{1,0:T(8,128)(2,1)} %tokens.3) | copy-start | bytes 6291460
  12.4 63.0 %all-to-all-start.4 = ((bf16[32,8,4224]{2,1,0:T(8,128)(2,1)}), bf16[32,8,4224]{2,1,0:T(8,128)(2,1)}, u32[]{:S(2)}, u32[]{:S(2)}) async-start(bf16[32,8,4224]{2,1,0:T(8,128)(2,1)} %bitcast.33), calls=%async_computation.4 | async-start | bytes 4325376 | tf_op jit(solution)/shard_map/all_to_all | solution.py:307
  24.2 30.4 %all-gather.2.cloned.1.call-start = ((), (), s32[]{:S(2)}) async-start(), calls=%async_computation.5 | async-start | bytes 1179648 | tf_op jit(solution)/shard_map/all_gather | solution.py:310
  54.5 1.2 copy-start
  75.4 6.6 %copy-start.4 = (f32[8192]{0:T(1024)S(1)}, f32[8192]{0:T(1024)}, u32[]{:S(2)}) copy-start(f32[8192]{0:T(1024)} %param.10) | copy-start | bytes 98308
  75.4 6.6 %copy-start.5 = (f32[128]{0:T(128)S(1)}, f32[128]{0:T(128)}, u32[]{:S(2)}) copy-start(f32[128]{0:T(128)} %param.12) | copy-start | bytes 1540
  75.4 57.6 %all-to-all-start.3 = ((bf16[32,8,4224]{2,1,0:T(8,128)(2,1)}), bf16[32,8,4224]{2,1,0:T(8,128)(2,1)}, u32[]{:S(2)}, u32[]{:S(2)}) async-start(bf16[32,8,4224]{2,1,0:T(8,128)(2,1)} %bitcast.32), calls=%async_computation.3 | async-start | bytes 4325376 | tf_op jit(solution)/shard_map/all_to_all | solution.py:307
  148.8 4.5 %collective-permute-start = (bf16[4,256,1024]{2,1,0:T(8,128)(2,1)}, bf16[4,256,1024]{2,1,0:T(8,128)(2,1)S(1)}, u32[]{:S(2)}, u32[]{:S(2)}) collective-permute-start(bf16[4,256,1024]{2,1,0:T(8,128)(2,1)} %get-tuple-element.23), channel_id=1, source_target_pairs={{0,32},{32,0},{64,96},{96,64},{128,160},{160,128},{192,224},{224,1... | collective-permute-start | bytes 6291464 | tf_op jit(solution)/shard_map/cond/branch_0_fun/ppermute | solution.py:359
Sparse Core Ops, SparseCore 0:
  27.5 27.0 all-gather.1

commit v3 on v2

--- a/solution.py
+++ b/solution.py
@@ -14,10 +14,14 @@
 HALVES = 2
 SLOTS = 4
 DIRECT = 2 * SLOTS
-LENT = 7
+LENT = 6
+PIECES = 8
 EXTRA = 128
 STRIDE = 16
-BIG = pltpu.CompilerParams(vmem_limit_bytes=52 * 2**20)
+
+
+def room(mib):
+    return pltpu.CompilerParams(vmem_limit_bytes=mib * 2**20)
 
 
 def mm(a, b):
@@ -60,9 +64,10 @@
 def first_kernel(lat_count, ids, home, tokens, chunk, lent):
     rows, width = tokens.shape
     part = width // HALVES
-    total = home.shape[0]
-    hit = iota((total, rows), 0) == ids[...]
-    places = jnp.sum(jnp.where(hit, home[...], 0), axis=0, keepdims=True)
+    total = home.shape[1]
+    hit = (iota((total, rows), 0) == ids[...]).astype(F32).astype(BF)
+    table = jnp.broadcast_to(home[...], (8, total)).astype(F32).astype(BF)
+    places = mm(table, hit)[:1].astype(I32)
     dest, block = places >> 1, places & 1
     unused, rank = ranks_of(dest, lat_count)
     rank = rank.astype(I32)
@@ -77,25 +82,27 @@
     chunk[:, part:] = jnp.broadcast_to(meta.astype(F32), (meta.shape[0], EXTRA)).astype(BF)
     over = (rank >= DIRECT).astype(F32)
     order = mm(jnp.broadcast_to(over, (8, rows)).astype(BF), before(rows))[:1]
-    list_row = iota((LENT + 1, rows), 0)
-    take = jnp.logical_and(order.astype(I32) == list_row, over > 0.5)
-    take = jnp.logical_and(take, list_row < LENT)
-    take = jnp.where(take, 1.0, 0.0).astype(BF)
-    for i in range(width // step):
-        got = mm(take, tokens[:, i * step : (i + 1) * step])
-        if i == 0:
-            head = jnp.where(list_row == LENT, places.astype(F32), got[:, :rows])
-            got = jnp.concatenate([head, got[:, rows:]], axis=1)
-        lent[:, i * step : (i + 1) * step] = got.astype(BF)
+    lines = (LENT + 1) * PIECES
+    line = iota((lines, rows), 0)
+    take = jnp.logical_and(order.astype(I32) == line // PIECES, over > 0.5)
+    take = jnp.where(jnp.logical_and(take, line < LENT * PIECES), 1.0, 0.0)
+    piece = iota((lines, 1), 0) % PIECES
+    got = jnp.zeros((lines, width // PIECES), F32)
+    for i in range(PIECES):
+        chosen = jnp.where(piece == i, take, 0.0).astype(BF)
+        got = got + mm(chosen, tokens[:, i * step : (i + 1) * step])
+    head = jnp.where(line == LENT * PIECES, places.astype(F32), got[:, :rows])
+    lent[...] = jnp.concatenate([head, got[:, rows:]], axis=1).astype(BF)
 
 
 def second_kernel(lat_count, group, tokens, loans, chunk, left):
     rows, width = tokens.shape
     part = width // HALVES
-    groups = loans.shape[0] // (LENT + 1)
+    lines = (LENT + 1) * PIECES
+    groups = loans.shape[0] // lines
     me = group[0]
-    heads = loans[:, :rows].astype(F32).reshape(groups, LENT + 1, rows)
-    places = heads[:, LENT, :].astype(I32)
+    heads = loans[:, :rows].astype(F32).reshape(groups, lines, rows)
+    places = heads[:, LENT * PIECES, :].astype(I32)
     dest, block = places >> 1, places & 1
     members, rank_f = ranks_of(dest, lat_count)
     rank = rank_f.astype(I32)
@@ -129,14 +136,14 @@
     here = jnp.logical_and(placed, jnp.logical_and(at >= 0, at < look(my_free)))
     slot = look(my_used) + at
     lent_code = jnp.where(here, (dest * STRIDE + slot) * 2 + block, -1)
-    list_row = iota((LENT + 1, rows), 0)
+    list_row = iota((lines, rows), 0) // PIECES
     columns = []
     for t in range(groups):
         chosen = jnp.logical_and(order[t : t + 1] == list_row, listed[t : t + 1])
         value = jnp.sum(jnp.where(chosen, lent_code[t : t + 1] + 1, 0), axis=1, keepdims=True) - 1
         columns.append(value)
     column = jnp.concatenate(columns, axis=0)
-    size = groups * (LENT + 1)
+    size = groups * lines
     lent_row = jnp.sum(
         jnp.where(iota((size, size), 0) == iota((size, size), 1), column, 0), axis=0, keepdims=True
     )
@@ -149,14 +156,16 @@
     codes, half = slot_codes(lat_count, SLOTS)
     low, high, meta = pick(codes, half, own_code)
     low2, high2, meta2 = pick(codes, half, lent_row)
+    meta2 = meta2 // PIECES
     both = jnp.concatenate([low, high], axis=1)
-    both2 = jnp.concatenate([low2, high2], axis=1)
+    low2, high2 = low2.astype(F32), high2.astype(F32)
+    piece = iota((1, size), 1) % PIECES
     step = 1024
     for i in range(part // step):
         lo, hi = slice(i * step, (i + 1) * step), slice(part + i * step, part + (i + 1) * step)
         own = jnp.concatenate([tokens[:, lo], tokens[:, hi]], axis=0)
-        other = jnp.concatenate([loans[:, lo], loans[:, hi]], axis=0)
-        chunk[:, lo] = (mm(both, own) + mm(both2, other)).astype(BF)
+        both2 = jnp.where(piece == i, low2, 0.0) + jnp.where(piece == i + part // step, high2, 0.0)
+        chunk[:, lo] = (mm(both, own) + mm(both2.astype(BF), loans[...])).astype(BF)
     code = (meta + meta2).astype(F32) + 4.0 * flag
     chunk[:, part:] = jnp.broadcast_to(code, (code.shape[0], EXTRA)).astype(BF)
 
@@ -294,13 +303,13 @@
 
     chunk1, lent = pl.pallas_call(
         functools.partial(first_kernel, lat_count),
-        out_shape=[chunk_shape, jax.ShapeDtypeStruct((LENT + 1, width), BF)],
+        out_shape=[chunk_shape, jax.ShapeDtypeStruct(((LENT + 1) * PIECES, width // PIECES), BF)],
         in_specs=[vmem()] * 3,
         out_specs=[vmem()] * 2,
-        compiler_params=BIG,
+        compiler_params=room(16),
         cost_estimate=move_cost,
         name="first_slots",
-    )(block_ids.reshape(1, rows), block_home.reshape(-1, 1), tokens)
+    )(block_ids.reshape(1, rows), block_home.reshape(1, -1), tokens)
 
     def exchange(chunk):
         shaped = chunk.reshape(lat_count, HALVES * SLOTS, part + EXTRA)
@@ -314,7 +323,7 @@
         out_shape=[chunk_shape, jax.ShapeDtypeStruct((8, rows), I32)],
         in_specs=[smem(), vmem(), vmem()],
         out_specs=[vmem()] * 2,
-        compiler_params=BIG,
+        compiler_params=room(24),
         cost_estimate=move_cost,
         name="second_slots",
     )(me.reshape(1), tokens, loans)
@@ -333,7 +342,7 @@
         in_specs=[vmem()] * 5,
         out_specs=vmem(),
         scratch_shapes=work,
-        compiler_params=BIG,
+        compiler_params=room(26),
         cost_estimate=matmul_cost,
         name="chunk_gradients",
     )
@@ -350,7 +359,7 @@
         in_specs=[smem()] + [vmem()] * 6,
         out_specs=[vmem()] * 3,
         scratch_shapes=work,
-        compiler_params=BIG,
+        compiler_params=room(32),
         cost_estimate=matmul_cost,
         name="last_gradients",
     )(core.reshape(1), got2, enc_weight, dec_weight, bias_row, offset_row, parts)
@@ -365,19 +374,23 @@
         total = jnp.sum(terms.astype(F32), axis=0)
         return total[:latents], total[latents:]
 
-    def with_rest(mine, other):
+    def rest(carry):
+        mine, other, unused = carry
         codes, half = slot_codes(lat_count, DIRECT)
         low, high, meta = pick(codes, half, left[:1])
         data = mm(low, tokens[:, :part]) + mm(high, tokens[:, part:])
         extra = jnp.broadcast_to(meta.astype(F32), (slot_rows, EXTRA))
         chunk3 = jnp.concatenate([data, extra], axis=1).astype(BF)
-        rest = part_call(exchange(chunk3), enc_weight, dec_weight, bias_row, offset_row)
-        rest = rest.reshape(half_groups, 2, 2 * latents, out_width)
-        mine = mine + lax.dynamic_index_in_dim(rest, core, 1, keepdims=False)
-        more = lax.dynamic_index_in_dim(rest, 1 - core, 1, keepdims=False)
-        return finish(mine, (other.astype(F32) + more).astype(BF))
-
-    return lax.cond(flags[0, 0] >= 4.0, with_rest, finish, mine, other)
+        more = part_call(exchange(chunk3), enc_weight, dec_weight, bias_row, offset_row)
+        more = more.reshape(half_groups, 2, 2 * latents, out_width)
+        mine = mine + lax.dynamic_index_in_dim(more, core, 1, keepdims=False)
+        more = lax.dynamic_index_in_dim(more, 1 - core, 1, keepdims=False)
+        return mine, (other.astype(F32) + more).astype(BF), jnp.zeros((), F32)
+
+    mine, other, unused = lax.while_loop(
+        lambda carry: carry[2] >= 4.0, rest, (mine, other, flags[0, 0])
+    )
+    return finish(mine, other)
 
 
 def solution(mesh):

time: 198 us -> 184 us (0.929)
  waiting for transfers between devices: 91 us -> 76.6 us
  blocking collectives: 30.9 us -> 45 us
  between operations: 14.7 us -> 0.76 us
  local copies, waits for them, and re-layouts: 5.41 us -> 12.2 us
  Pallas kernels: 32.8 us -> 26.4 us
    all_gather x1 -> x0, waiting for transfers between devices: 29.6 us -> none  [on_device(): loans = lax.all_gather(lent, 'tok', tiled=True)]
    all_to_all x2, waiting for transfers between devices: 56.4 us -> 72.2 us  [exchange(): got = lax.all_to_all(shaped, 'lat', split_axis=0, concat_axis=0, tiled=True)]
    all_gather x0 -> x1, blocking collectives: none -> 14 us  [on_device(): loans = lax.all_gather(lent, 'tok', tiled=True)]
    unnamed x10 -> x16, local copies, waits for them, and re-layouts: 1.89 us -> 10.6 us
    pallas_call x1, Pallas kernels: 10.8 us -> 6.93 us  [on_device(): parts = part_call(got1, enc_weight, dec_weight, bias_row, offset_row)]
    pallas_call x1, Pallas kernels: 14.7 us -> 12.2 us  [on_device(): pl.pallas_call(last_kernel, out_shape=[jax.ShapeDtypeStruct((half_groups,...]
  transfers between devices with their start and end apart: 4 -> 3, of which waited for: 4 -> 3; matrix products, arithmetic and copies ran while one was open for 0% -> 0% of each run, Pallas kernels for 7% -> 6%
where the time goes in v3:
time: 184 us; the launch traced here: 183 us
  waiting for transfers between devices  76.6 us (42%)
  blocking collectives  45 us (24%)
  Pallas kernels  26.4 us (14%)
  starting transfers between devices  18.2 us (10%)
  local copies, waits for them, and re-layouts  12.2 us (7%)
  other arithmetic  3.32 us (2%)
    all_to_all x2, waiting for transfers between devices, exchange(): got = lax.all_to_all(shaped, 'lat', split_axis=0, concat_axis=0, tiled=True)  72.2 us
    all_to_all x1, blocking collectives, finish(): lax.all_to_all(summed, 'tok', split_axis=0, concat_axis=0, tiled=True, ax...  30.9 us
    all_to_all x2, starting transfers between devices, exchange(): got = lax.all_to_all(shaped, 'lat', split_axis=0, concat_axis=0, tiled=True)  18.1 us
    all_gather x1, blocking collectives, on_device(): loans = lax.all_gather(lent, 'tok', tiled=True)  14 us
    pallas_call x1, Pallas kernels, on_device(): pl.pallas_call(last_kernel, out_shape=[jax.ShapeDtypeStruct((half_groups,...  12.2 us
    unnamed x16, local copies, waits for them, and re-layouts  10.6 us
    pallas_call x1, Pallas kernels, on_device(): parts = part_call(got1, enc_weight, dec_weight, bias_row, offset_row)  6.93 us
    ppermute x1, waiting for transfers between devices, finish(): swapped = lax.ppermute(other, 'tok', [(i, i ^ 1) for i in range(groups)])  4.36 us
  transfers between devices with their start and end apart: 3, of which 3 were waited for; matrix products, arithmetic and copies ran while one was open for 0% of the time, Pallas kernels for 6%

profile of v3, /device:TPU:6, one launch (start us, length us, event | category | flops | bytes accessed | tf_op | source)
XLA Modules:
  0.0 183.3 jit_solution(5739576408728098666)
XLA Ops:
  0.6 0.0 copy-start.4
  0.6 0.6 copy-done.4
  1.3 0.0 copy-start.5
  1.3 0.7 copy-done.5
  1.9 3.0 %first_slots.1 = (bf16[256,4224]{1,0:T(8,128)(2,1)S(1)}, bf16[56,1024]{1,0:T(8,128)(2,1)S(1)}) custom-call(s32[1,128]{1,0:T(1,128)S(1)} %bitcast.30, s32[1,64]{1,0:T(1,128)S(1)} %bitcast.31, bf16[128,8192]{1,0:T(8,128)(2,1)} %tokens.3), custom_call_target="tpu_custom_call" | custom-call | flops 536870912 | bytes 5242880 | tf_op jit(solution)/shard_map/first_slots/pallas_call | solution.py:304
  4.9 0.0 copy-start.3
  4.9 1.3 copy-done.3
  6.3 11.6 %all-to-all-start.2 = ((bf16[32,8,4224]{2,1,0:T(8,128)(2,1)}), bf16[32,8,4224]{2,1,0:T(8,128)(2,1)S(1)}, u32[]{:S(2)}, u32[]{:S(2)}) async-start(bf16[32,8,4224]{2,1,0:T(8,128)(2,1)} %bitcast.29), calls=%async_computation.2 | async-start | bytes 4325376 | tf_op jit(solution)/shard_map/all_to_all | solution.py:316
  17.8 14.0 %all_gather.3.loans = bf16[448,1024]{1,0:T(8,128)(2,1)S(1)} all-gather(bf16[56,1024]{1,0:T(8,128)(2,1)S(1)} %get-tuple-element.61), channel_id=1, replica_groups=mesh['tok'=8,'lat'=32] {'tok'}, dimensions={0}, use_global_device_ids=true | all-gather | bytes 1032192 | tf_op jit(solution)/shard_map/all_gather | solution.py:319
  31.9 4.3 %second_slots.1 = (bf16[256,4224]{1,0:T(8,128)(2,1)S(1)}, s32[8,128]{1,0:T(8,128)S(1)}) custom-call(s32[1]{0:T(128)} %bitcast.8.group, bf16[128,8192]{1,0:T(8,128)(2,1)} %tokens.3, bf16[448,1024]{1,0:T(8,128)(2,1)S(1)} %all_gather.3.loans), custom_call_target="tpu_custom_call" | custom-call | flops 536870912 | bytes 5242880 | tf_op jit(solution)/shard_map/second_slots/pallas_call | solution.py:321
  36.2 0.0 copy-start.2
  36.2 1.3 copy-done.2
  37.6 31.4 %all-to-all-done.2 = bf16[32,8,4224]{2,1,0:T(8,128)(2,1)S(1)} async-done(((bf16[32,8,4224]{2,1,0:T(8,128)(2,1)}), bf16[32,8,4224]{2,1,0:T(8,128)(2,1)S(1)}, u32[]{:S(2)}, u32[]{:S(2)}) %all-to-all-start.2) | async-done | bytes 2162720 | tf_op jit(solution)/shard_map/all_to_all | solution.py:316
  69.0 0.0 copy-start.9
  69.0 0.0 copy-start.10
  69.0 6.5 %all-to-all-start.1 = ((bf16[32,8,4224]{2,1,0:T(8,128)(2,1)}), bf16[32,8,4224]{2,1,0:T(8,128)(2,1)}, u32[]{:S(2)}, u32[]{:S(2)}) async-start(bf16[32,8,4224]{2,1,0:T(8,128)(2,1)} %bitcast.28), calls=%async_computation.1 | async-start | bytes 4325376 | tf_op jit(solution)/shard_map/all_to_all | solution.py:316
  75.6 0.0 copy-done.9
  75.6 0.0 copy-done.10
  75.6 6.9 %chunk_gradients.3.parts = f32[8,256,1024]{2,1,0:T(8,128)S(1)} custom-call(bf16[256,4224]{1,0:T(8,128)(2,1)S(1)} %bitcast.27, bf16[128,8192]{1,0:T(8,128)(2,1)} %enc.3, bf16[128,8192]{1,0:T(8,128)(2,1)} %dec.3, f32[1,128]{1,0:T(1,128)S(1)} %bitcast.35, f32[1,8192]{1,0:T(1,128)S(1)} %bitcast.32), custom_call_target="tpu_custom_call" | custom-call | flops 2684354560 | bytes 16777216 | tf_op jit(solution)/shard_map/chunk_gradients/pallas_call | solution.py:349
  82.5 0.0 copy-start
  82.5 3.2 %copy-done = f32[8,256,1024]{2,1,0:T(8,128)} copy-done((f32[8,256,1024]{2,1,0:T(8,128)}, f32[8,256,1024]{2,1,0:T(8,128)S(1)}, u32[]{:S(2)}) %copy-start) | copy-done | bytes 8388632
  85.7 40.8 %all-to-all-done.1 = bf16[32,8,4224]{2,1,0:T(8,128)(2,1)} async-done(((bf16[32,8,4224]{2,1,0:T(8,128)(2,1)}), bf16[32,8,4224]{2,1,0:T(8,128)(2,1)}, u32[]{:S(2)}, u32[]{:S(2)}) %all-to-all-start.1) | async-done | bytes 2162720 | tf_op jit(solution)/shard_map/all_to_all | solution.py:316
  126.5 0.0 copy-start.1
  126.5 3.4 %copy-done.1 = f32[8,256,1024]{2,1,0:T(8,128)S(1)} copy-done((f32[8,256,1024]{2,1,0:T(8,128)S(1)}, f32[8,256,1024]{2,1,0:T(8,128)}, u32[]{:S(2)}) %copy-start.1) | copy-done | bytes 8388632
  129.9 12.2 %last_gradients.1 = (f32[4,256,1024]{2,1,0:T(8,128)}, bf16[4,256,1024]{2,1,0:T(8,128)(2,1)}, f32[8,128]{1,0:T(8,128)S(1)}) custom-call(s32[1]{0:T(128)} %bitcast.7.core, bf16[256,4224]{1,0:T(8,128)(2,1)} %bitcast.12.chunk, bf16[128,8192]{1,0:T(8,128)(2,1)} %enc.3, bf16[128,8192]{1,0:T(8,128)(2,1)} %dec.3, f32[1,128]{1,0:T(1,128)S(1)} %bitcast.36, ...), custom_call_target="tpu_custom_call" | custom-call | flops 2684354560 | bytes 16777216 | tf_op jit(solution)/shard_map/last_gradients/pallas_call | solution.py:352
  142.1 0.5 slice.18
  142.6 0.9 while.11
  143.5 0.1 collective-permute-start
  143.6 4.4 %collective-permute-done = bf16[4,256,1024]{2,1,0:T(8,128)(2,1)S(1)} collective-permute-done((bf16[4,256,1024]{2,1,0:T(8,128)(2,1)}, bf16[4,256,1024]{2,1,0:T(8,128)(2,1)S(1)}, u32[]{:S(2)}, u32[]{:S(2)}) %collective-permute-start) | collective-permute-done | bytes 2097184 | tf_op jit(solution)/shard_map/ppermute | solution.py:368
  148.0 3.0 %add_convert_fusion = bf16[4,256,1024]{2,1,0:T(8,128)(2,1)S(1)} fusion(f32[4,256,1024]{2,1,0:T(8,128)} %get-tuple-element.68, bf16[4,256,1024]{2,1,0:T(8,128)(2,1)S(1)} %collective-permute-done), kind=kLoop, calls=%fused_computation.51 | loop fusion | flops 3145728 | bytes 8388608 | tf_op jit(solution)/shard_map/convert_element_type | solution.py:369
  150.9 30.9 %all_to_all.19 = bf16[4,256,1024]{2,1,0:T(8,128)(2,1)S(1)} all-to-all(bf16[4,256,1024]{2,1,0:T(8,128)(2,1)S(1)} %add_convert_fusion), channel_id=1, replica_groups={{0,64,128,192},{32,96,160,224},{1,65,129,193},{33,97,161,225},{2,66,130..., dimensions={0} | all-to-all | bytes 4194304 | tf_op jit(solution)/shard_map/all_to_all | solution.py:371
  181.8 0.4 convert_reduce_fusion
  182.2 1.0 fusion.24
Async XLA Ops:
  0.6 0.7 copy-start.4
  1.3 0.7 copy-start.5
  4.9 1.3 copy-start.3
  6.3 62.7 %all-to-all-start.2 = ((bf16[32,8,4224]{2,1,0:T(8,128)(2,1)}), bf16[32,8,4224]{2,1,0:T(8,128)(2,1)S(1)}, u32[]{:S(2)}, u32[]{:S(2)}) async-start(bf16[32,8,4224]{2,1,0:T(8,128)(2,1)} %bitcast.29), calls=%async_computation.2 | async-start | bytes 4325376 | tf_op jit(solution)/shard_map/all_to_all | solution.py:316
  36.2 1.4 copy-start.2
  69.0 6.6 %copy-start.9 = (f32[8192]{0:T(1024)S(1)}, f32[8192]{0:T(1024)}, u32[]{:S(2)}) copy-start(f32[8192]{0:T(1024)} %param.10) | copy-start | bytes 98308
  69.0 6.6 %copy-start.10 = (f32[128]{0:T(128)S(1)}, f32[128]{0:T(128)}, u32[]{:S(2)}) copy-start(f32[128]{0:T(128)} %param.12) | copy-start | bytes 1540
  69.0 57.6 %all-to-all-start.1 = ((bf16[32,8,4224]{2,1,0:T(8,128)(2,1)}), bf16[32,8,4224]{2,1,0:T(8,128)(2,1)}, u32[]{:S(2)}, u32[]{:S(2)}) async-start(bf16[32,8,4224]{2,1,0:T(8,128)(2,1)} %bitcast.28), calls=%async_computation.1 | async-start | bytes 4325376 | tf_op jit(solution)/shard_map/all_to_all | solution.py:316
  82.5 3.2 %copy-start = (f32[8,256,1024]{2,1,0:T(8,128)}, f32[8,256,1024]{2,1,0:T(8,128)S(1)}, u32[]{:S(2)}) copy-start(f32[8,256,1024]{2,1,0:T(8,128)S(1)} %chunk_gradients.3.parts) | copy-start | bytes 25165828
  126.5 3.4 %copy-start.1 = (f32[8,256,1024]{2,1,0:T(8,128)S(1)}, f32[8,256,1024]{2,1,0:T(8,128)}, u32[]{:S(2)}) copy-start(f32[8,256,1024]{2,1,0:T(8,128)} %copy-done) | copy-start | bytes 25165828
  143.5 4.5 %collective-permute-start = (bf16[4,256,1024]{2,1,0:T(8,128)(2,1)}, bf16[4,256,1024]{2,1,0:T(8,128)(2,1)S(1)}, u32[]{:S(2)}, u32[]{:S(2)}) collective-permute-start(bf16[4,256,1024]{2,1,0:T(8,128)(2,1)} %get-tuple-element.69), channel_id=1, source_target_pairs={{0,32},{32,0},{64,96},{96,64},{128,160},{160,128},{192,224},{224,1... | collective-permute-start | bytes 6291464 | tf_op jit(solution)/shard_map/ppermute | solution.py:368

commit v4 on v3

--- a/solution.py
+++ b/solution.py
@@ -14,7 +14,7 @@
 HALVES = 2
 SLOTS = 4
 DIRECT = 2 * SLOTS
-LENT = 6
+LENT = 7
 PIECES = 8
 EXTRA = 128
 STRIDE = 16
@@ -61,7 +61,7 @@
     return members, jnp.sum(members * counts, axis=1)
 
 
-def first_kernel(lat_count, ids, home, tokens, chunk, lent):
+def first_kernel(lat_count, ids, home, tokens, chunk, lent, heads):
     rows, width = tokens.shape
     part = width // HALVES
     total = home.shape[1]
@@ -82,27 +82,26 @@
     chunk[:, part:] = jnp.broadcast_to(meta.astype(F32), (meta.shape[0], EXTRA)).astype(BF)
     over = (rank >= DIRECT).astype(F32)
     order = mm(jnp.broadcast_to(over, (8, rows)).astype(BF), before(rows))[:1]
-    lines = (LENT + 1) * PIECES
+    lines = LENT * PIECES
     line = iota((lines, rows), 0)
     take = jnp.logical_and(order.astype(I32) == line // PIECES, over > 0.5)
-    take = jnp.where(jnp.logical_and(take, line < LENT * PIECES), 1.0, 0.0)
+    take = jnp.where(take, 1.0, 0.0)
     piece = iota((lines, 1), 0) % PIECES
     got = jnp.zeros((lines, width // PIECES), F32)
     for i in range(PIECES):
         chosen = jnp.where(piece == i, take, 0.0).astype(BF)
         got = got + mm(chosen, tokens[:, i * step : (i + 1) * step])
-    head = jnp.where(line == LENT * PIECES, places.astype(F32), got[:, :rows])
-    lent[...] = jnp.concatenate([head, got[:, rows:]], axis=1).astype(BF)
-
-
-def second_kernel(lat_count, group, tokens, loans, chunk, left):
+    lent[...] = got.astype(BF)
+    heads[...] = jnp.broadcast_to(places, heads.shape)
+
+
+def second_kernel(lat_count, group, tokens, loans, heads, chunk, left):
     rows, width = tokens.shape
     part = width // HALVES
-    lines = (LENT + 1) * PIECES
+    lines = LENT * PIECES
     groups = loans.shape[0] // lines
     me = group[0]
-    heads = loans[:, :rows].astype(F32).reshape(groups, lines, rows)
-    places = heads[:, LENT * PIECES, :].astype(I32)
+    places = heads[...].reshape(groups, heads.shape[0] // groups, rows)[:, 0, :]
     dest, block = places >> 1, places & 1
     members, rank_f = ranks_of(dest, lat_count)
     rank = rank_f.astype(I32)
@@ -170,7 +169,7 @@
     chunk[:, part:] = jnp.broadcast_to(code, (code.shape[0], EXTRA)).astype(BF)
 
 
-def gradient_body(chunk, enc, dec, bias, dec_bias, cent, err, acc, store):
+def gradient_body(chunk, enc, dec, bias, dec_bias, cent, err, acc, store, ready):
     rows, padded = chunk.shape
     part = padded - EXTRA
     latents = enc.shape[0]
@@ -202,6 +201,7 @@
 
     for i in range(steps):
         lo, hi = pair(i)
+        ready("first", i)
         x = chunk[:, lo].astype(F32).reshape(rows // group, group, step)
         c = (x - offset(i)).reshape(rows, step).astype(BF)
         cent[:, lo] = c
@@ -210,6 +210,7 @@
             acc[...] = mm_t(c, w)
         else:
             acc[...] += mm_t(c, w)
+    ready("code", 0)
     code = chunk[:, part:].astype(F32)
     code = jnp.where(code >= 4.0, code - 4.0, code)
     second = iota((1, latents), 1) >= latents // 2
@@ -218,6 +219,7 @@
     gate = 1.0 / (1.0 + jnp.exp(-pre))
     latent = spread(jnp.where(valid, pre * gate, 0.0))
     latent_b = latent.astype(BF)
+    ready("second", 0)
     for i in range(steps):
         lo, hi = pair(i)
         w = jnp.concatenate([dec[:, lo], dec[:, hi]], axis=0)
@@ -233,6 +235,7 @@
     dpre = spread(jnp.where(valid, dlatent * gate * (1.0 + pre * (1.0 - gate)), 0.0))
     dpre_t = dpre.T.astype(BF)
     latent_t = latent.T.astype(BF)
+    ready("third", 0)
     for i in range(steps):
         lo, hi = pair(i)
         store(i, 0, mm(dpre_t, cent[:, lo]))
@@ -248,14 +251,71 @@
         parts[i, rows] = value[:latents]
         parts[steps + i, rows] = value[latents:]
 
-    gradient_body(chunk, enc, dec, bias, dec_bias, cent, err, acc, store)
+    gradient_body(
+        chunk, enc, dec, bias, dec_bias, cent, err, acc, store, lambda stage, i: None
+    )
 
 
 def last_kernel(
-    core, chunk, enc, dec, bias, dec_bias, parts, mine, other, flags, cent, err, acc
+    core,
+    chunk_in,
+    enc_in,
+    dec_in,
+    bias,
+    dec_bias,
+    parts_in,
+    mine_out,
+    other_out,
+    flags,
+    chunk,
+    enc,
+    dec,
+    parts,
+    mine,
+    other,
+    cent,
+    err,
+    acc,
+    sems_in,
+    sems_out,
 ):
     latents = enc.shape[0]
     steps = parts.shape[0] // HALVES
+    part = chunk.shape[1] - EXTRA
+    step = part // steps
+    moves = {}
+
+    def move(key, source, target):
+        moves[key] = pltpu.make_async_copy(source, target, sems_in.at[len(moves)])
+        moves[key].start()
+
+    for i in range(steps):
+        lo = pl.ds(i * step, step)
+        move(("chunk", i), chunk_in.at[:, lo], chunk.at[:, lo])
+        for h in range(HALVES):
+            cols = pl.ds(h * part + i * step, step)
+            move(("enc", i, h), enc_in.at[:, cols], enc.at[:, cols])
+    tail = pl.ds(part, EXTRA)
+    move("code", chunk_in.at[:, tail], chunk.at[:, tail])
+    move("dec", dec_in, dec)
+    move("parts", parts_in, parts)
+
+    def ready(stage, i):
+        if stage == "first":
+            moves[("chunk", i)].wait()
+            for h in range(HALVES):
+                moves[("enc", i, h)].wait()
+        elif stage == "code":
+            moves["code"].wait()
+        elif stage == "second":
+            moves["dec"].wait()
+        else:
+            moves["parts"].wait()
+
+    def out_copy(which, place):
+        source, target = ((mine, mine_out), (other, other_out))[which]
+        sem = sems_out.at[which * steps + place]
+        return pltpu.make_async_copy(source.at[place], target.at[place], sem)
 
     def store(i, grad, value):
         rows = slice(grad * latents, (grad + 1) * latents)
@@ -266,18 +326,29 @@
             @pl.when(core[0] == k % 2)
             def _():
                 mine[k // 2, rows] = total
+                if grad == 1:
+                    out_copy(0, k // 2).start()
 
             @pl.when(core[0] != k % 2)
             def _():
                 other[k // 2, rows] = total.astype(BF)
-
-    top = jnp.max(chunk[:, chunk.shape[1] - EXTRA :].astype(F32), axis=0, keepdims=True)
+                if grad == 1:
+                    out_copy(1, k // 2).start()
+
+    gradient_body(chunk, enc, dec, bias, dec_bias, cent, err, acc, store, ready)
+    top = jnp.max(chunk[:, part:].astype(F32), axis=0, keepdims=True)
     flags[...] = jnp.broadcast_to(top, flags.shape)
-    gradient_body(chunk, enc, dec, bias, dec_bias, cent, err, acc, store)
+    for which in range(2):
+        for place in range(steps):
+            out_copy(which, place).wait()
 
 
 def vmem():
     return pl.BlockSpec(memory_space=pltpu.VMEM)
+
+
+def anywhere():
+    return pl.BlockSpec(memory_space=pl.ANY)
 
 
 def smem():
@@ -301,11 +372,15 @@
         flops=2 * slot_rows * 2 * rows * part, bytes_accessed=5 * 2**20, transcendentals=0
     )
 
-    chunk1, lent = pl.pallas_call(
+    chunk1, lent, heads = pl.pallas_call(
         functools.partial(first_kernel, lat_count),
-        out_shape=[chunk_shape, jax.ShapeDtypeStruct(((LENT + 1) * PIECES, width // PIECES), BF)],
+        out_shape=[
+            chunk_shape,
+            jax.ShapeDtypeStruct((LENT * PIECES, width // PIECES), BF),
+            jax.ShapeDtypeStruct((8, rows), I32),
+        ],
         in_specs=[vmem()] * 3,
-        out_specs=[vmem()] * 2,
+        out_specs=[vmem()] * 3,
         compiler_params=room(16),
         cost_estimate=move_cost,
         name="first_slots",
@@ -316,17 +391,19 @@
         got = lax.all_to_all(shaped, "lat", split_axis=0, concat_axis=0, tiled=True)
         return got.reshape(slot_rows, part + EXTRA)
 
+    heads = lax.all_gather(heads, "tok", tiled=True)
+    lent, heads = lax.optimization_barrier((lent, heads))
     loans = lax.all_gather(lent, "tok", tiled=True)
     got1 = exchange(chunk1)
     chunk2, left = pl.pallas_call(
         functools.partial(second_kernel, lat_count),
         out_shape=[chunk_shape, jax.ShapeDtypeStruct((8, rows), I32)],
-        in_specs=[smem(), vmem(), vmem()],
+        in_specs=[smem(), vmem(), vmem(), vmem()],
         out_specs=[vmem()] * 2,
         compiler_params=room(24),
         cost_estimate=move_cost,
         name="second_slots",
-    )(me.reshape(1), tokens, loans)
+    )(me.reshape(1), tokens, loans, heads)
     got2 = exchange(chunk2)
 
     bias_row = enc_bias.reshape(1, latents)
@@ -342,7 +419,7 @@
         in_specs=[vmem()] * 5,
         out_specs=vmem(),
         scratch_shapes=work,
-        compiler_params=room(26),
+        compiler_params=room(56),
         cost_estimate=matmul_cost,
         name="chunk_gradients",
     )
@@ -356,10 +433,20 @@
             jax.ShapeDtypeStruct((half_groups, 2 * latents, out_width), BF),
             jax.ShapeDtypeStruct((8, EXTRA), F32),
         ],
-        in_specs=[smem()] + [vmem()] * 6,
-        out_specs=[vmem()] * 3,
-        scratch_shapes=work,
-        compiler_params=room(32),
+        in_specs=[smem()] + [anywhere()] * 3 + [vmem()] * 2 + [anywhere()],
+        out_specs=[anywhere()] * 2 + [vmem()],
+        scratch_shapes=[
+            pltpu.VMEM((slot_rows, part + EXTRA), BF),
+            pltpu.VMEM((latents, width), BF),
+            pltpu.VMEM((latents, width), BF),
+            pltpu.VMEM((groups, 2 * latents, out_width), F32),
+            pltpu.VMEM((half_groups, 2 * latents, out_width), F32),
+            pltpu.VMEM((half_groups, 2 * latents, out_width), BF),
+            *work,
+            pltpu.SemaphoreType.DMA((3 * half_groups + 3,)),
+            pltpu.SemaphoreType.DMA((2 * half_groups,)),
+        ],
+        compiler_params=room(56),
         cost_estimate=matmul_cost,
         name="last_gradients",
     )(core.reshape(1), got2, enc_weight, dec_weight, bias_row, offset_row, parts)

time: 184 us -> 179 us (0.973)
  blocking collectives: 45 us -> 57.8 us
  waiting for transfers between devices: 76.6 us -> 64.7 us
  local copies, waits for them, and re-layouts: 12.2 us -> 3.56 us
  Pallas kernels: 26.4 us -> 29.3 us
    all_gather x0 -> x1, blocking collectives: none -> 13.3 us  [on_device(): heads = lax.all_gather(heads, 'tok', tiled=True)]
    all_to_all x2, waiting for transfers between devices: 72.2 us -> 60.3 us  [exchange(): got = lax.all_to_all(shaped, 'lat', split_axis=0, concat_axis=0, tiled=True)]
    unnamed x16 -> x10, local copies, waits for them, and re-layouts: 10.6 us -> 1.31 us
    pallas_call x1, Pallas kernels: 6.93 us -> 10.9 us  [on_device(): parts = part_call(got1, enc_weight, dec_weight, bias_row, offset_row)]
    pallas_call x1, Pallas kernels: 12.2 us -> 10.4 us  [on_device(): pl.pallas_call(last_kernel, out_shape=[jax.ShapeDtypeStruct((half_groups,...]
  transfers between devices with their start and end apart: 3 -> 3, of which waited for: 3 -> 3; matrix products, arithmetic and copies ran while one was open for 0% -> 0% of each run, Pallas kernels for 6% -> 8%
where the time goes in v4:
time: 179 us
  waiting for transfers between devices  64.7 us (36%)
  blocking collectives  57.8 us (32%)
  Pallas kernels  29.3 us (16%)
  starting transfers between devices  18.4 us (10%)
  local copies, waits for them, and re-layouts  3.56 us (2%)
  other arithmetic  3.44 us (2%)
    all_to_all x2, waiting for transfers between devices, exchange(): got = lax.all_to_all(shaped, 'lat', split_axis=0, concat_axis=0, tiled=True)  60.3 us
    all_to_all x1, blocking collectives, finish(): lax.all_to_all(summed, 'tok', split_axis=0, concat_axis=0, tiled=True, ax...  30.9 us
    all_to_all x2, starting transfers between devices, exchange(): got = lax.all_to_all(shaped, 'lat', split_axis=0, concat_axis=0, tiled=True)  18.3 us
    all_gather x1, blocking collectives, on_device(): loans = lax.all_gather(lent, 'tok', tiled=True)  13.5 us
    all_gather x1, blocking collectives, on_device(): heads = lax.all_gather(heads, 'tok', tiled=True)  13.3 us
    pallas_call x1, Pallas kernels, on_device(): parts = part_call(got1, enc_weight, dec_weight, bias_row, offset_row)  10.9 us
    pallas_call x1, Pallas kernels, on_device(): pl.pallas_call(last_kernel, out_shape=[jax.ShapeDtypeStruct((half_groups,...  10.4 us
    ppermute x1, waiting for transfers between devices, finish(): swapped = lax.ppermute(other, 'tok', [(i, i ^ 1) for i in range(groups)])  4.36 us
  transfers between devices with their start and end apart: 3, of which 3 were waited for; matrix products, arithmetic and copies ran while one was open for 0% of the time, Pallas kernels for 8%

profile of v4, /device:TPU:6, one launch (start us, length us, event | category | flops | bytes accessed | tf_op | source)
XLA Modules:
  0.0 178.6 jit_solution(5318211152428673821)
XLA Ops:
  0.6 0.0 copy-start
  0.6 0.6 copy-done
  1.3 0.0 copy-start.1
  1.3 0.7 copy-done.1
  1.9 3.9 %first_slots.1 = (bf16[256,4224]{1,0:T(8,128)(2,1)}, bf16[56,1024]{1,0:T(8,128)(2,1)S(1)}, s32[8,128]{1,0:T(8,128)S(1)}) custom-call(s32[1,128]{1,0:T(1,128)S(1)} %bitcast.25, s32[1,64]{1,0:T(1,128)S(1)} %bitcast.26, bf16[128,8192]{1,0:T(8,128)(2,1)} %tokens.3), custom_call_target="tpu_custom_call" | custom-call | flops 536870912 | bytes 5242880 | tf_op jit(solution)/shard_map/first_slots/pallas_call | solution.py:375
  5.9 0.0 copy-start.5
  5.9 11.7 %all-to-all-start.2 = ((bf16[32,8,4224]{2,1,0:T(8,128)(2,1)}), bf16[32,8,4224]{2,1,0:T(8,128)(2,1)}, u32[]{:S(2)}, u32[]{:S(2)}) async-start(bf16[32,8,4224]{2,1,0:T(8,128)(2,1)} %bitcast.15), calls=%async_computation.2 | async-start | bytes 4325376 | tf_op jit(solution)/shard_map/all_to_all | solution.py:391
  17.6 13.3 %all_gather.6.heads = s32[64,128]{1,0:T(8,128)S(1)} all-gather(s32[8,128]{1,0:T(8,128)S(1)} %get-tuple-element.65), channel_id=1, replica_groups=mesh['tok'=8,'lat'=32] {'tok'}, dimensions={0}, use_global_device_ids=true | all-gather | bytes 36864 | tf_op jit(solution)/shard_map/all_gather | solution.py:394
  31.0 13.5 %all_gather.7.loans = bf16[448,1024]{1,0:T(8,128)(2,1)S(1)} all-gather(bf16[56,1024]{1,0:T(8,128)(2,1)S(1)} %get-tuple-element.66), channel_id=1, replica_groups=mesh['tok'=8,'lat'=32] {'tok'}, dimensions={0}, use_global_device_ids=true | all-gather | bytes 1032192 | tf_op jit(solution)/shard_map/all_gather | solution.py:396
  44.5 0.0 copy-done.5
  44.5 4.1 %second_slots.1 = (bf16[256,4224]{1,0:T(8,128)(2,1)}, s32[8,128]{1,0:T(8,128)S(1)}) custom-call(s32[1]{0:T(128)} %bitcast.8.group, bf16[128,8192]{1,0:T(8,128)(2,1)S(1)} %copy-done.5, bf16[448,1024]{1,0:T(8,128)(2,1)S(1)} %all_gather.7.loans, s32[64,128]{1,0:T(8,128)S(1)} %all_gather.6.heads), custom_call_target="tpu_custom_call" | custom-call | flops 536870912 | bytes 5242880 | tf_op jit(solution)/shard_map/second_slots/pallas_call | solution.py:398
  48.6 20.3 %all-to-all-done.2 = bf16[32,8,4224]{2,1,0:T(8,128)(2,1)} async-done(((bf16[32,8,4224]{2,1,0:T(8,128)(2,1)}), bf16[32,8,4224]{2,1,0:T(8,128)(2,1)}, u32[]{:S(2)}, u32[]{:S(2)}) %all-to-all-start.2) | async-done | bytes 2162720 | tf_op jit(solution)/shard_map/all_to_all | solution.py:391
  68.8 0.0 copy-start.7
  68.8 0.0 copy-start.8
  68.8 6.5 %all-to-all-start.1 = ((bf16[32,8,4224]{2,1,0:T(8,128)(2,1)}), bf16[32,8,4224]{2,1,0:T(8,128)(2,1)}, u32[]{:S(2)}, u32[]{:S(2)}) async-start(bf16[32,8,4224]{2,1,0:T(8,128)(2,1)} %bitcast.11), calls=%async_computation.1 | async-start | bytes 4325376 | tf_op jit(solution)/shard_map/all_to_all | solution.py:391
  75.4 0.0 copy-done.7
  75.4 0.0 copy-done.8
  75.4 10.9 %chunk_gradients.3.parts_in = f32[8,256,1024]{2,1,0:T(8,128)} custom-call(bf16[256,4224]{1,0:T(8,128)(2,1)} %bitcast.16.chunk, bf16[128,8192]{1,0:T(8,128)(2,1)} %enc_in.1, bf16[128,8192]{1,0:T(8,128)(2,1)} %dec_in.1, f32[1,128]{1,0:T(1,128)S(1)} %bitcast.32, f32[1,8192]{1,0:T(1,128)S(1)} %bitcast.29), custom_call_target="tpu_custom_call" | custom-call | flops 2684354560 | bytes 16777216 | tf_op jit(solution)/shard_map/chunk_gradients/pallas_call | solution.py:426
  86.3 40.1 %all-to-all-done.1 = bf16[32,8,4224]{2,1,0:T(8,128)(2,1)} async-done(((bf16[32,8,4224]{2,1,0:T(8,128)(2,1)}), bf16[32,8,4224]{2,1,0:T(8,128)(2,1)}, u32[]{:S(2)}, u32[]{:S(2)}) %all-to-all-start.1) | async-done | bytes 2162720 | tf_op jit(solution)/shard_map/all_to_all | solution.py:391
  126.4 10.4 %last_gradients.1 = (f32[4,256,1024]{2,1,0:T(8,128)}, bf16[4,256,1024]{2,1,0:T(8,128)(2,1)}, f32[8,128]{1,0:T(8,128)}) custom-call(s32[1]{0:T(128)} %bitcast.7.core, bf16[256,4224]{1,0:T(8,128)(2,1)} %bitcast.12.chunk_in, bf16[128,8192]{1,0:T(8,128)(2,1)} %enc_in.1, bf16[128,8192]{1,0:T(8,128)(2,1)} %dec_in.1, f32[1,128]{1,0:T(1,128)S(1)} %bitcast.33, ...), custom_call_target="tpu_custom_call" | custom-call | flops 2684354560 | bytes 16777216 | tf_op jit(solution)/shard_map/last_gradients/pallas_call | solution.py:429
  136.8 1.2 slice.18
  138.0 0.8 while.11
  138.8 0.1 collective-permute-start
  138.9 4.4 %collective-permute-done = bf16[4,256,1024]{2,1,0:T(8,128)(2,1)S(1)} collective-permute-done((bf16[4,256,1024]{2,1,0:T(8,128)(2,1)}, bf16[4,256,1024]{2,1,0:T(8,128)(2,1)S(1)}, u32[]{:S(2)}, u32[]{:S(2)}) %collective-permute-start) | collective-permute-done | bytes 2097184 | tf_op jit(solution)/shard_map/ppermute | solution.py:455
  143.2 3.0 %add_convert_fusion = bf16[4,256,1024]{2,1,0:T(8,128)(2,1)S(1)} fusion(f32[4,256,1024]{2,1,0:T(8,128)} %get-tuple-element.145, bf16[4,256,1024]{2,1,0:T(8,128)(2,1)S(1)} %collective-permute-done), kind=kLoop, calls=%fused_computation.51 | loop fusion | flops 3145728 | bytes 8388608 | tf_op jit(solution)/shard_map/convert_element_type | solution.py:456
  146.3 30.9 %all_to_all.19 = bf16[4,256,1024]{2,1,0:T(8,128)(2,1)S(1)} all-to-all(bf16[4,256,1024]{2,1,0:T(8,128)(2,1)S(1)} %add_convert_fusion), channel_id=1, replica_groups={{0,64,128,192},{32,96,160,224},{1,65,129,193},{33,97,161,225},{2,66,130..., dimensions={0} | all-to-all | bytes 4194304 | tf_op jit(solution)/shard_map/all_to_all | solution.py:458
  177.2 0.4 convert_reduce_fusion
  177.6 1.0 fusion.24
Async XLA Ops:
  0.6 0.7 copy-start
  1.3 0.7 copy-start.1
  5.9 38.6 %copy-start.5 = (bf16[128,8192]{1,0:T(8,128)(2,1)S(1)}, bf16[128,8192]{1,0:T(8,128)(2,1)}, u32[]{:S(2)}) copy-start(bf16[128,8192]{1,0:T(8,128)(2,1)} %tokens.3) | copy-start | bytes 6291460
  5.9 63.0 %all-to-all-start.2 = ((bf16[32,8,4224]{2,1,0:T(8,128)(2,1)}), bf16[32,8,4224]{2,1,0:T(8,128)(2,1)}, u32[]{:S(2)}, u32[]{:S(2)}) async-start(bf16[32,8,4224]{2,1,0:T(8,128)(2,1)} %bitcast.15), calls=%async_computation.2 | async-start | bytes 4325376 | tf_op jit(solution)/shard_map/all_to_all | solution.py:391
  68.8 6.6 %copy-start.7 = (f32[8192]{0:T(1024)S(1)}, f32[8192]{0:T(1024)}, u32[]{:S(2)}) copy-start(f32[8192]{0:T(1024)} %param.10) | copy-start | bytes 98308
  68.8 6.6 %copy-start.8 = (f32[128]{0:T(128)S(1)}, f32[128]{0:T(128)}, u32[]{:S(2)}) copy-start(f32[128]{0:T(128)} %param.12) | copy-start | bytes 1540
  68.8 57.6 %all-to-all-start.1 = ((bf16[32,8,4224]{2,1,0:T(8,128)(2,1)}), bf16[32,8,4224]{2,1,0:T(8,128)(2,1)}, u32[]{:S(2)}, u32[]{:S(2)}) async-start(bf16[32,8,4224]{2,1,0:T(8,128)(2,1)} %bitcast.11), calls=%async_computation.1 | async-start | bytes 4325376 | tf_op jit(solution)/shard_map/all_to_all | solution.py:391
  138.8 4.5 %collective-permute-start = (bf16[4,256,1024]{2,1,0:T(8,128)(2,1)}, bf16[4,256,1024]{2,1,0:T(8,128)(2,1)S(1)}, u32[]{:S(2)}, u32[]{:S(2)}) collective-permute-start(bf16[4,256,1024]{2,1,0:T(8,128)(2,1)} %get-tuple-element.146), channel_id=1, source_target_pairs={{0,32},{32,0},{64,96},{96,64},{128,160},{160,128},{192,224},{224,1... | collective-permute-start | bytes 6291464 | tf_op jit(solution)/shard_map/ppermute | solution.py:455
